TPU v7x, 256 devices: a whole 4x4x8 slice. The times are simulated.
256 devices in a mesh: replica: 8 (over z), dp: 8 (over x_lo, y), section: 4 (over x_hi, core).
Axes of the slice: x: 4 (x_hi: 2, x_lo: 2; x = x_hi * 2 + x_lo), y: 4, z: 8, core: 2. Of those that a mesh axis runs over, the one named last changes fastest.
Arguments:
- activations: bfloat16 [8, 4, 3072, 4096], P('replica', 'section', 'dp'), may hold values from -0.4375 to 0.4375
- key_cotangent: bfloat16 [8, 4, 3072, 1024], P('replica', 'section', 'dp'), may hold values from -6 to 6
- key_weight: bfloat16 [8, 4, 4096, 1024], P('replica', 'section', 'dp'), may hold values from -0.09375 to 0.09375
- delta_codes: bfloat16 [8, 4, 4096, 1024], P('replica', 'section', 'dp'), may hold values from -127 to 127, as said below
- delta_exponents: int32 [8, 4, 4096, 8], P('replica', 'section', 'dp'), may hold values from -10 to -6
- outer_momentum: float32 [4, 4096, 1024], P('section', ('dp', 'replica')), may hold values from -6 to 6
- outer_master: float32 [4, 4096, 1024], P('section', ('dp', 'replica')), may hold values from -6 to 6
Outputs:
- sent_cotangent: bfloat16 [8, 4, 3072, 4096], P('replica', 'section', 'dp')
- weight_grad: bfloat16 [8, 4, 4096, 1024], P('replica', 'section', 'dp')
- momentum_new: float32 [4, 4096, 1024], P('section', ('dp', 'replica'))
- master_new: float32 [4, 4096, 1024], P('section', ('dp', 'replica'))
- synced_weight: bfloat16 [4, 4096, 1024], P('section', 'dp')
Inputs may be any that keep to these rules, and one draw needn't show every extreme that they name: delta_codes holds whole numbers.
All inputs are finite; a program needn't handle non-finite values.
Results may differ from a plain program's by a relative error of at most 0.017.
Values may be sent and summed in bfloat16 or wider, within the bound.
No kernel may reach another device: no remote copies, remote signals or barrier semaphores. Data moves between devices by JAX's collectives and lax.ppermute only.
A program may use at most 128 MiB of HBM per device.

v0:
```python
import jax
import jax.numpy as jnp
from jax import lax
from jax.sharding import PartitionSpec as P


def shifted(value, axis, steps):
    count = lax.axis_size(axis)
    first, last = (max(0, -steps), min(count, count - steps))
    return lax.ppermute(value, axis, [(source, source + steps) for source in range(first, last)])


def body(
    activations,
    key_cotangent,
    key_weight,
    delta_codes,
    delta_exponents,
    outer_momentum,
    outer_master,
):
    features = activations[0, 0]
    cotang = key_cotangent[0, 0]
    weights = key_weight[0, 0]
    own_rows = weights.shape[0]
    width = weights.shape[1]
    input_grad = lax.dot_general(
        cotang,
        lax.all_gather(weights, "dp", axis=0, tiled=True),
        (((1,), (1,)), ((), ())),
        preferred_element_type=jnp.float32,
    ).astype(jnp.bfloat16)
    grad_sum = lax.psum_scatter(
        lax.dot_general(
            features, cotang, (((0,), (0,)), ((), ())), preferred_element_type=jnp.float32
        ).astype(jnp.bfloat16),
        "dp",
        scatter_dimension=0,
        tiled=True,
    )
    sent = shifted(input_grad, "section", -1)
    sent_cotangent = sent[None, None]
    weight_grad = grad_sum[None, None]
    codes = delta_codes[0, 0].astype(jnp.float32)
    scales = jnp.exp2(delta_exponents[0, 0].astype(jnp.float32))
    blocks = scales.shape[1]
    delta = (codes.reshape(own_rows, blocks, width // blocks) * scales[..., None]).reshape(
        own_rows, width
    )
    total = lax.psum_scatter(
        delta.astype(jnp.bfloat16), "replica", scatter_dimension=0, tiled=True
    ).astype(jnp.float32)
    mean_delta = total / lax.axis_size("replica")
    momentum_new = 0.9 * outer_momentum[0] + mean_delta
    master_new = outer_master[0] - 0.7 * (mean_delta + 0.9 * momentum_new)
    synced = lax.all_gather(master_new.astype(jnp.bfloat16), "replica", axis=0, tiled=True)
    return (sent_cotangent, weight_grad, momentum_new[None], master_new[None], synced[None])


def solution(mesh):
    placed = (
        P("replica", "section", "dp", None),
        P("replica", "section", "dp", None),
        P("replica", "section", "dp", None),
        P("replica", "section", "dp", None),
        P("replica", "section", "dp", None),
        P("section", ("dp", "replica"), None),
        P("section", ("dp", "replica"), None),
    )
    return jax.shard_map(
        body,
        mesh=mesh,
        in_specs=placed,
        out_specs=(
            P("replica", "section", "dp", None),
            P("replica", "section", "dp", None),
            P("section", ("dp", "replica"), None),
            P("section", ("dp", "replica"), None),
            P("section", "dp", None),
        ),
        check_vma=False,
    )
```

profile of v0, /device:TPU:1, one launch (start us, length us, event | category | flops | bytes accessed | tf_op | source)
XLA Modules:
  0.0 261.9 jit_solution(16253020814350020783)
XLA Ops:
  8.0 0.0 copy-start
  8.0 0.0 reduce-scatter.5.cloned.1.call-start
  8.1 0.9 exponential_bitcast_fusion
  8.9 0.1 copy.12
  9.1 0.6 mul.28
  9.7 0.0 copy-start.2
  9.7 2.8 %fusion.6 = bf16[512,1024]{1,0:T(8,128)(2,1)} fusion(f32[64,8,8,128]{3,2,1,0:T(8,128)S(1)} %bitcast.46, bf16[1,1,512,1024]{3,2,1,0:T(8,128)(2,1)} %param.10), kind=kLoop, calls=%fused_computation.6 | loop fusion | flops 1572864 | bytes 4194304 | tf_op jit(solution)/shard_map/convert_element_type | solution.py:51
  12.5 0.0 reduce-scatter.5.cloned.1.call-update
  12.5 0.0 all-gather.6.cloned.1.call-start
  12.6 0.5 all-gather.6.cloned.1.call-update
  13.1 0.0 all-gather.4.cloned.1.call-start
  13.2 38.3 %reduce-scatter.5.cloned.1.call-done = bf16[64,1024]{1,0:T(8,128)(2,1)} async-done(((bf16[512,1024]{1,0:T(8,128)(2,1)}), bf16[64,1024]{1,0:T(8,128)(2,1)}) %reduce-scatter.5.cloned.1.call-update) | async-done | bytes 131088 | tf_op jit(solution)/shard_map/reduce_scatter | solution.py:50
  51.4 0.0 copy-done.2
  51.4 1.9 fusion.10
  53.4 0.0 all-gather.4.cloned.1.call-update
  53.4 0.0 reduce-scatter.3.cloned.1.call-start
  53.5 0.0 copy-done
  53.5 7.9 %convolution_convert_fusion = bf16[4096,1024]{1,0:T(8,128)(2,1)} fusion(bf16[1,1,384,4096]{3,2,1,0:T(8,128)(2,1)S(1)} %copy-done, bf16[1,1,384,1024]{3,2,1,0:T(8,128)(2,1)} %param.8), kind=kOutput, calls=%fused_computation.2 | convolution fusion | flops 3225419776 | bytes 12320768 | tf_op jit(solution)/shard_map/dot_general | solution.py:34
  61.3 0.0 reduce-scatter.3.cloned.1.call-update
  61.3 51.6 %all-gather.6.cloned.1.call-done = bf16[1,1,4096,1024]{3,2,1,0:T(8,128)(2,1)} async-done(((bf16[1,1,512,1024]{3,2,1,0:T(8,128)(2,1)}), bf16[1,1,4096,1024]{3,2,1,0:T(8,128)(2,1)}) %all-gather.6.cloned.1.call-update) | async-done | bytes 8388624 | tf_op jit(solution)/shard_map/all_gather | solution.py:29
  112.9 8.8 %fusion.2 = bf16[384,4096]{1,0:T(8,128)(2,1)} fusion(bf16[1,1,4096,1024]{3,2,1,0:T(8,128)(2,1)} %all-gather.6.cloned.1.call-done, bf16[1,1,384,1024]{3,2,1,0:T(8,128)(2,1)} %param.8), kind=kOutput, calls=%fused_computation.3 | convolution fusion | flops 3222798336 | bytes 12320768 | tf_op jit(solution)/shard_map/dot_general | solution.py:27
  121.7 2.7 %collective-permute-start = (bf16[384,4096]{1,0:T(8,128)(2,1)}, bf16[384,4096]{1,0:T(8,128)(2,1)}, u32[]{:S(2)}, u32[]{:S(2)}) collective-permute-start(bf16[384,4096]{1,0:T(8,128)(2,1)} %fusion.2), channel_id=1, source_target_pairs={{1,0},{2,1},{3,2},{5,4},{6,5},{7,6},{9,8},{10,9},{11,10},{13,12},{... | collective-permute-start | bytes 9437192 | tf_op jit(solution)/shard_map/ppermute | solution.py:10
  124.4 23.3 %all-gather.4.cloned.1.call-done = bf16[512,1024]{1,0:T(8,128)(2,1)} async-done(((bf16[64,1024]{1,0:T(8,128)(2,1)}), bf16[512,1024]{1,0:T(8,128)(2,1)}) %all-gather.4.cloned.1.call-update) | async-done | bytes 1048592 | tf_op jit(solution)/shard_map/all_gather | solution.py:56
  147.7 14.4 %collective-permute-done = bf16[384,4096]{1,0:T(8,128)(2,1)} collective-permute-done((bf16[384,4096]{1,0:T(8,128)(2,1)}, bf16[384,4096]{1,0:T(8,128)(2,1)}, u32[]{:S(2)}, u32[]{:S(2)}) %collective-permute-start) | collective-permute-done | bytes 3145760 | tf_op jit(solution)/shard_map/ppermute | solution.py:10
  162.1 87.2 %reduce-scatter.3.cloned.1.call-done = bf16[512,1024]{1,0:T(8,128)(2,1)} async-done(((bf16[4096,1024]{1,0:T(8,128)(2,1)}), bf16[512,1024]{1,0:T(8,128)(2,1)}) %reduce-scatter.3.cloned.1.call-update) | async-done | bytes 1048592 | tf_op jit(solution)/shard_map/reduce_scatter | solution.py:33
  249.3 0.0 copy-start.1
  249.3 4.0 %copy.17 = bf16[1,1,384,4096]{3,2,1,0:T(8,128)(2,1)} copy(bf16[1,1,384,4096]{3,2,1,0:T(8,128)(2,1)} %bitcast.2) | data formatting | bytes 6291456
  253.3 0.0 copy-done.1
  253.3 1.0 copy.18
Async XLA Ops:
  8.0 45.5 %copy-start = (bf16[1,1,384,4096]{3,2,1,0:T(8,128)(2,1)S(1)}, bf16[1,1,384,4096]{3,2,1,0:T(8,128)(2,1)}, u32[]{:S(2)}) copy-start(bf16[1,1,384,4096]{3,2,1,0:T(8,128)(2,1)} %param.7) | copy-start | bytes 9437188
  8.0 43.4 %reduce-scatter.5.cloned.1.call-start = ((), (), s32[]{:S(2)}) async-start(), calls=%async_computation.3 | async-start | bytes 1179648 | tf_op jit(solution)/shard_map/reduce_scatter | solution.py:50
  9.7 41.8 %copy-start.2 = (f32[1,64,1024]{2,1,0:T(8,128)S(1)}, f32[1,64,1024]{2,1,0:T(8,128)}, u32[]{:S(2)}) copy-start(f32[1,64,1024]{2,1,0:T(8,128)} %param.12) | copy-start | bytes 786436
  12.5 100.4 %all-gather.6.cloned.1.call-start = ((), (), s32[]{:S(2)}) async-start(), calls=%async_computation.5 | async-start | bytes 9437184 | tf_op jit(solution)/shard_map/all_gather | solution.py:29
  13.1 134.6 %all-gather.4.cloned.1.call-start = ((), (), s32[]{:S(2)}) async-start(), calls=%async_computation.4 | async-start | bytes 1179648 | tf_op jit(solution)/shard_map/all_gather | solution.py:56
  53.4 195.9 %reduce-scatter.3.cloned.1.call-start = ((), (), s32[]{:S(2)}) async-start(), calls=%async_computation.2 | async-start | bytes 9437184 | tf_op jit(solution)/shard_map/reduce_scatter | solution.py:33
  121.7 40.4 %collective-permute-start = (bf16[384,4096]{1,0:T(8,128)(2,1)}, bf16[384,4096]{1,0:T(8,128)(2,1)}, u32[]{:S(2)}, u32[]{:S(2)}) collective-permute-start(bf16[384,4096]{1,0:T(8,128)(2,1)} %fusion.2), channel_id=1, source_target_pairs={{1,0},{2,1},{3,2},{5,4},{6,5},{7,6},{9,8},{10,9},{11,10},{13,12},{... | collective-permute-start | bytes 9437192 | tf_op jit(solution)/shard_map/ppermute | solution.py:10
  249.3 4.0 %copy-start.1 = (bf16[512,1024]{1,0:T(8,128)(2,1)S(1)}, bf16[512,1024]{1,0:T(8,128)(2,1)}, u32[]{:S(2)}) copy-start(bf16[512,1024]{1,0:T(8,128)(2,1)} %all-gather.4.cloned.1.call-done) | copy-start | bytes 3145732
Sparse Core Ops, SparseCore 0:
  12.6 38.7 reduce-scatter.4
Sparse Core Ops, SparseCore 1:
  14.8 98.1 all-gather.5
  115.2 32.5 all-gather.3
  150.7 98.5 reduce-scatter.2
where the time goes:
time: 262 us
  waiting for transfers between devices  215 us (82%)
  matrix products  16.6 us (6%)
  between operations  15.7 us (6%)
  local copies, waits for them, and re-layouts  5.72 us (2%)
  other arithmetic  5.63 us (2%)
  starting transfers between devices  2.84 us (1%)
    reduce_scatter x1, waiting for transfers between devices, body(): lax.psum_scatter(lax.dot_general(features, cotang, (((0,), (0,)), ((), ()...  87.2 us
    all_gather x1, waiting for transfers between devices, body(): lax.all_gather(weights, 'dp', axis=0, tiled=True)  51.6 us
    reduce_scatter x1, waiting for transfers between devices, body(): lax.psum_scatter(delta.astype(jnp.bfloat16), 'replica', scatter_dimension...  38.3 us
    all_gather x1, waiting for transfers between devices, body(): lax.all_gather(master_new.astype(jnp.bfloat16), 'replica', axis=0, tiled=...  23.3 us
    ppermute x1, waiting for transfers between devices, shifted(): lax.ppermute(value, axis, [(source, source + steps) for source in range(f...  14.4 us
    dot_general x1, matrix products, body(): lax.dot_general(cotang, lax.all_gather(weights, 'dp', axis=0, tiled=True)...  8.75 us
    dot_general x1, matrix products, body(): lax.dot_general(features, cotang, (((0,), (0,)), ((), ())), preferred_ele...  7.85 us
  transfers between devices with their start and end apart: 5, of which 5 were waited for; matrix products, arithmetic and copies ran while one was open for 7% of the time, Pallas kernels for 0%

commit v1 on v0

v1 whole, which is shorter than its diff:
```python
import jax
import jax.numpy as jnp
from jax import lax
from jax.sharding import PartitionSpec as P

NX, NY = 2, 4


def solution(mesh):
    sections = mesh.shape["section"]
    replicas = mesh.shape["replica"]

    def moved(value, to, first=0):
        pairs = []
        for x in range(NX):
            for y in range(NY):
                for s in range(first, sections):
                    tx, ty, ts = to(x, y, s)
                    if 0 <= ts < sections:
                        source = (x * NY + y) * sections + s
                        target = (tx % NX * NY + ty % NY) * sections + ts
                        pairs.append((source, target))
        return lax.ppermute(value, ("dp", "section"), pairs)

    def body(act, cot, w, codes, exps, mom, mas):
        act, cot, w, codes, exps, mom, mas = (
            act[0, 0], cot[0, 0], w[0, 0], codes[0, 0], exps[0, 0], mom[0], mas[0])
        rows, width = w.shape
        half = NY * rows
        tok = act.shape[0]
        dp = lax.axis_index("dp")
        x, y = dp // NY, dp % NY

        with jax.named_scope("pair_swap"):
            cot_o = moved(cot, lambda x, y, s: (x + 1, y, s))
            act_o = moved(
                lax.dynamic_slice(act, (0, (1 - x) * half), (tok, half)),
                lambda x, y, s: (x + 1, y, s))
        with jax.named_scope("gather_weight"):
            ws = [w] + [moved(w, lambda x, y, s, r=r: (x, y - r, s), 1) for r in (1, 2, 3)]

        with jax.named_scope("outer"):
            scales = jnp.exp2(exps.astype(jnp.float32))
            blocks = scales.shape[1]
            delta = codes.astype(jnp.float32).reshape(rows, blocks, width // blocks) * scales[..., None]
            delta = delta.reshape(replicas, rows // replicas, width).astype(jnp.bfloat16)
            delta = lax.all_to_all(delta, "replica", 0, 0)
            mean = jnp.sum(delta.astype(jnp.float32), axis=0) / replicas
            mom_new = 0.9 * mom + mean
            mas_new = mas - 0.7 * (mean + 0.9 * mom_new)
            synced = lax.all_gather(mas_new.astype(jnp.bfloat16), "replica", axis=0, tiled=True)

        with jax.named_scope("input_grad"):
            def grads(c):
                return jnp.stack([lax.dot_general(
                    c, b, (((1,), (1,)), ((), ())), preferred_element_type=jnp.float32
                ).astype(jnp.bfloat16) for b in ws])
            other = moved(grads(cot_o), lambda x, y, s: (x + 1, y, s - 1), 1)
            own = moved(grads(cot), lambda x, y, s: (x, y, s - 1), 1)

        with jax.named_scope("weight_grad"):
            own_half = lax.dynamic_slice(act, (0, x * half), (tok, half))
            pair_act = jnp.concatenate([own_half, act_o], 0)
            pair_cot = jnp.concatenate([cot, cot_o], 0)
            parts = []
            for r in (2, 1, 3, 0):
                block = lax.dynamic_slice(pair_act, (0, (y + r) % NY * rows), (2 * tok, rows))
                parts.append(lax.dot_general(
                    block, pair_cot, (((0,), (0,)), ((), ())), preferred_element_type=jnp.float32))
            grad = parts[3]
            for r, part in zip((2, 1, 3), parts):
                grad = grad + moved(
                    part.astype(jnp.bfloat16), lambda x, y, s, r=r: (x, y + r, s)).astype(jnp.float32)
            grad = grad.astype(jnp.bfloat16)

        with jax.named_scope("assemble"):
            def placed(blocks):
                flat = jnp.concatenate([blocks, blocks], 0)
                flat = lax.dynamic_slice(flat, ((NY - y) % NY, 0, 0), blocks.shape)
                return jnp.concatenate(list(flat), 1)
            own, other = placed(own), placed(other)
            sent = jnp.where(x == 0, jnp.concatenate([own, other], 1), jnp.concatenate([other, own], 1))
        return (sent[None, None], grad[None, None], mom_new[None], mas_new[None], synced[None])

    placed = (
        P("replica", "section", "dp", None),
        P("replica", "section", "dp", None),
        P("replica", "section", "dp", None),
        P("replica", "section", "dp", None),
        P("replica", "section", "dp", None),
        P("section", ("dp", "replica"), None),
        P("section", ("dp", "replica"), None),
    )
    return jax.shard_map(
        body,
        mesh=mesh,
        in_specs=placed,
        out_specs=(
            P("replica", "section", "dp", None),
            P("replica", "section", "dp", None),
            P("section", ("dp", "replica"), None),
            P("section", ("dp", "replica"), None),
            P("section", "dp", None),
        ),
        check_vma=False,
    )
```

time: 262 us -> 149 us (0.57)
  the two profiles are of different devices: /device:TPU:1 before, /device:TPU:4 now
where the time goes in v1:
time: 149 us; the launch traced here: 148 us
  waiting for transfers between devices  40.8 us (27%)
  starting transfers between devices  33.6 us (23%)
  matrix products  28.5 us (19%)
  other arithmetic  19.5 us (13%)
  between operations  14.5 us (10%)
  local copies, waits for them, and re-layouts  11.2 us (8%)
    ppermute x10, waiting for transfers between devices, moved(): return lax.ppermute(value, ('dp', 'section'), pairs)  36.4 us
    ppermute x10, starting transfers between devices, moved(): return lax.ppermute(value, ('dp', 'section'), pairs)  25.1 us
    dot_general x8, matrix products, grads(): lax.dot_general(c, b, (((1,), (1,)), ((), ())), preferred_element_type=jn...  15.6 us
    dot_general x4, matrix products, body(): lax.dot_general(block, pair_cot, (((0,), (0,)), ((), ())), preferred_elem...  12.9 us
    all_to_all x1, starting transfers between devices, body(): delta = lax.all_to_all(delta, 'replica', 0, 0)  8.47 us
    mul x2, local copies, waits for them, and re-layouts, body(): codes.astype(jnp.float32).reshape(rows, blocks, width // blocks)  4.65 us
    all_gather x1, waiting for transfers between devices, body(): lax.all_gather(mas_new.astype(jnp.bfloat16), 'replica', axis=0, tiled=True)  4.43 us
    concatenate x2, other arithmetic, placed(): flat = jnp.concatenate([blocks, blocks], 0)  3.94 us
  transfers between devices with their start and end apart: 12, of which 6 were waited for; matrix products, arithmetic and copies ran while one was open for 38% of the time, Pallas kernels for 0%

profile of v1, /device:TPU:4, one launch (start us, length us, event | category | flops | bytes accessed | tf_op | source)
XLA Modules:
  0.0 148.0 jit_solution(10689803267003203584)
XLA Ops:
  7.2 3.5 %collective-permute-start.2 = (bf16[512,1024]{1,0:T(8,128)(2,1)}, bf16[512,1024]{1,0:T(8,128)(2,1)}, u32[]{:S(2)}, u32[]{:S(2)}) collective-permute-start(bf16[512,1024]{1,0:T(8,128)(2,1)} %bitcast.128), channel_id=1, source_target_pairs={{1,5},{2,6},{3,7},{5,9},{6,10},{7,11},{9,13},{10,14},{11,15},{13,1... | collective-permute-start | bytes 3145736 | tf_op jit(solution)/shard_map/gather_weight/ppermute | solution.py:23
  10.7 3.6 %collective-permute-start = (bf16[512,1024]{1,0:T(8,128)(2,1)}, bf16[512,1024]{1,0:T(8,128)(2,1)}, u32[]{:S(2)}, u32[]{:S(2)}) collective-permute-start(bf16[512,1024]{1,0:T(8,128)(2,1)} %bitcast.129), channel_id=1, source_target_pairs={{1,13},{2,14},{3,15},{5,1},{6,2},{7,3},{9,5},{10,6},{11,7},{13,9},... | collective-permute-start | bytes 3145736 | tf_op jit(solution)/shard_map/gather_weight/ppermute | solution.py:23
  14.2 3.9 %collective-permute-start.1 = (bf16[512,1024]{1,0:T(8,128)(2,1)}, bf16[512,1024]{1,0:T(8,128)(2,1)}, u32[]{:S(2)}, u32[]{:S(2)}) collective-permute-start(bf16[512,1024]{1,0:T(8,128)(2,1)} %bitcast.130), channel_id=1, source_target_pairs={{1,9},{2,10},{3,11},{5,13},{6,14},{7,15},{9,1},{10,2},{11,3},{13,5... | collective-permute-start | bytes 3145736 | tf_op jit(solution)/shard_map/gather_weight/ppermute | solution.py:23
  19.4 3.5 %dynamic-slice_bitcast_fusion = (bf16[384,2048]{1,0:T(8,128)(2,1)}, bf16[384,2048]{1,0:T(8,128)(2,1)S(1)}) fusion(bf16[1,1,384,4096]{3,2,1,0:T(8,128)(2,1)} %param.7, s32[]{:T(128)S(6)} %select_n.77, s32[]{:T(128)S(6)} %select_n.76), kind=kLoop, calls=%fused_computation.22 | loop fusion | bytes 6291464 | tf_op jit(solution)/shard_map/pair_swap/dynamic_slice | solution.py:37
  23.9 1.9 %mul.61 = f32[512,8,128]{2,1,0:T(8,128)} broadcast(f32[512,8]{1,0:T(8,128)S(1)} %copy.12), dimensions={0,1} | broadcast | bytes 2113536 | tf_op jit(solution)/shard_map/outer/mul | solution.py:45
  25.8 2.7 %mul.62 = f32[8,64,1024]{2,1,0:T(8,128)} reshape(f32[512,8,128]{2,1,0:T(8,128)} %mul.61) | data formatting | bytes 4194304 | tf_op jit(solution)/shard_map/outer/mul | solution.py:45
  28.5 3.2 %fusion = bf16[8,64,1024]{2,1,0:T(8,128)(2,1)} fusion(f32[8,64,1024]{2,1,0:T(8,128)} %mul.62, bf16[8,64,1024]{2,1,0:T(8,128)(2,1)} %bitcast.127), kind=kLoop, calls=%fused_computation.14 | loop fusion | flops 1572864 | bytes 4194304 | tf_op jit(solution)/shard_map/outer/convert_element_type | solution.py:46
  31.7 8.5 %all-to-all-start = ((bf16[8,64,1024]{2,1,0:T(8,128)(2,1)}), bf16[8,64,1024]{2,1,0:T(8,128)(2,1)}, u32[]{:S(2)}, u32[]{:S(2)}) async-start(bf16[8,64,1024]{2,1,0:T(8,128)(2,1)} %fusion), calls=%async_computation | async-start | bytes 2097152 | tf_op jit(solution)/shard_map/outer/all_to_all | solution.py:47
  40.3 2.2 %fusion.3 = bf16[1,384,512]{2,1,0:T(8,128)(2,1)S(1)} fusion(bf16[1,1,512,1024]{3,2,1,0:T(8,128)(2,1)} %param.9, bf16[1,1,384,1024]{3,2,1,0:T(8,128)(2,1)} %param.8), kind=kOutput, calls=%fused_computation.35 | convolution fusion | flops 402849792 | bytes 2228224 | tf_op jit(solution)/shard_map/input_grad/dot_general | solution.py:55
  42.5 1.7 %fusion.7 = bf16[1,384,512]{2,1,0:T(8,128)(2,1)S(1)} fusion(bf16[384,1024]{1,0:T(8,128)(2,1)} %collective-permute-done.4, bf16[1,1,512,1024]{3,2,1,0:T(8,128)(2,1)S(1)} %copy-done.5), kind=kOutput, calls=%fused_computation.39 | convolution fusion | flops 402849792 | bytes 2228224 | tf_op jit(solution)/shard_map/input_grad/dot_general | solution.py:55
  44.3 2.1 %fusion.10 = bf16[1,384,512]{2,1,0:T(8,128)(2,1)S(1)} fusion(bf16[384,1024]{1,0:T(8,128)(2,1)} %collective-permute-done.4, bf16[512,1024]{1,0:T(8,128)(2,1)} %collective-permute-done.2), kind=kOutput, calls=%fused_computation.42 | convolution fusion | flops 402849792 | bytes 2228224 | tf_op jit(solution)/shard_map/input_grad/dot_general | solution.py:55
  46.4 2.1 %fusion.8 = bf16[1,384,512]{2,1,0:T(8,128)(2,1)S(1)} fusion(bf16[384,1024]{1,0:T(8,128)(2,1)} %collective-permute-done.4, bf16[512,1024]{1,0:T(8,128)(2,1)} %collective-permute-done), kind=kOutput, calls=%fused_computation.40 | convolution fusion | flops 402849792 | bytes 2228224 | tf_op jit(solution)/shard_map/input_grad/dot_general | solution.py:55
  48.4 10.8 %collective-permute-done.1 = bf16[512,1024]{1,0:T(8,128)(2,1)} collective-permute-done((bf16[512,1024]{1,0:T(8,128)(2,1)}, bf16[512,1024]{1,0:T(8,128)(2,1)}, u32[]{:S(2)}, u32[]{:S(2)}) %collective-permute-start.1) | collective-permute-done | bytes 1048608 | tf_op jit(solution)/shard_map/gather_weight/ppermute | solution.py:23
  59.2 2.1 %fusion.9 = bf16[1,384,512]{2,1,0:T(8,128)(2,1)S(1)} fusion(bf16[384,1024]{1,0:T(8,128)(2,1)} %collective-permute-done.4, bf16[512,1024]{1,0:T(8,128)(2,1)} %collective-permute-done.1), kind=kOutput, calls=%fused_computation.41 | convolution fusion | flops 402849792 | bytes 2228224 | tf_op jit(solution)/shard_map/input_grad/dot_general | solution.py:55
  62.7 1.9 %collective-permute-start.5 = (bf16[4,384,512]{2,1,0:T(8,128)(2,1)}, bf16[4,384,512]{2,1,0:T(8,128)(2,1)}, u32[]{:S(2)}, u32[]{:S(2)}) collective-permute-start(bf16[4,384,512]{2,1,0:T(8,128)(2,1)} %pad_maximum_fusion.1), channel_id=1, source_target_pairs={{1,16},{2,17},{3,18},{5,20},{6,21},{7,22},{9,24},{10,25},{11,26},{... | collective-permute-start | bytes 4718600 | tf_op jit(solution)/shard_map/input_grad/ppermute | solution.py:23
  64.6 1.8 %fusion.4 = bf16[1,384,512]{2,1,0:T(8,128)(2,1)S(1)} fusion(bf16[512,1024]{1,0:T(8,128)(2,1)} %collective-permute-done, bf16[1,1,384,1024]{3,2,1,0:T(8,128)(2,1)S(1)} %copy-done), kind=kOutput, calls=%fused_computation.36 | convolution fusion | flops 402849792 | bytes 2228224 | tf_op jit(solution)/shard_map/input_grad/dot_general | solution.py:55
  66.4 1.8 %fusion.5 = bf16[1,384,512]{2,1,0:T(8,128)(2,1)S(1)} fusion(bf16[512,1024]{1,0:T(8,128)(2,1)} %collective-permute-done.1, bf16[1,1,384,1024]{3,2,1,0:T(8,128)(2,1)S(1)} %copy-done), kind=kOutput, calls=%fused_computation.37 | convolution fusion | flops 402849792 | bytes 2228224 | tf_op jit(solution)/shard_map/input_grad/dot_general | solution.py:55
  68.3 1.8 %fusion.6 = bf16[1,384,512]{2,1,0:T(8,128)(2,1)S(1)} fusion(bf16[512,1024]{1,0:T(8,128)(2,1)} %collective-permute-done.2, bf16[1,1,384,1024]{3,2,1,0:T(8,128)(2,1)S(1)} %copy-done), kind=kOutput, calls=%fused_computation.38 | convolution fusion | flops 402849792 | bytes 2228224 | tf_op jit(solution)/shard_map/input_grad/dot_general | solution.py:55
  71.5 1.9 %collective-permute-start.3 = (bf16[4,384,512]{2,1,0:T(8,128)(2,1)}, bf16[4,384,512]{2,1,0:T(8,128)(2,1)}, u32[]{:S(2)}, u32[]{:S(2)}) collective-permute-start(bf16[4,384,512]{2,1,0:T(8,128)(2,1)} %pad_maximum_fusion), channel_id=1, source_target_pairs={{1,0},{2,1},{3,2},{5,4},{6,5},{7,6},{9,8},{10,9},{11,10},{13,12},{... | collective-permute-start | bytes 4718600 | tf_op jit(solution)/shard_map/input_grad/ppermute | solution.py:23
  73.4 3.2 %convolution_convert_fusion.2 = bf16[512,1024]{1,0:T(8,128)(2,1)} fusion(s32[]{:T(128)S(6)} %select_n.81, bf16[384,2048]{1,0:T(8,128)(2,1)S(1)} %get-tuple-element.8, bf16[384,2048]{1,0:T(8,128)(2,1)S(1)} %collective-permute-done.6, bf16[384,1024]{1,0:T(8,128)(2,1)} %collective-permute-done.4, bf16[384,1024]{1,0:T(8,128)(2,1)S(1)} %bitcast.122), kind=kOutput, calls=%fused_computation.26 | convolution fusion | flops 810549248 | bytes 5767172 | tf_op jit(solution)/shard_map/weight_grad/dot_general | solution.py:68
  76.6 4.9 %collective-permute-start.7 = (bf16[512,1024]{1,0:T(8,128)(2,1)}, bf16[512,1024]{1,0:T(8,128)(2,1)}, u32[]{:S(2)}, u32[]{:S(2)}) collective-permute-start(bf16[512,1024]{1,0:T(8,128)(2,1)} %convolution_convert_fusion.2), channel_id=1, source_target_pairs={{0,8},{1,9},{2,10},{3,11},{4,12},{5,13},{6,14},{7,15},{8,0},{9,1},... | collective-permute-start | bytes 3145736 | tf_op jit(solution)/shard_map/weight_grad/ppermute | solution.py:23
  81.5 3.1 %convolution_convert_fusion.1 = bf16[512,1024]{1,0:T(8,128)(2,1)} fusion(s32[]{:T(128)S(6)} %select_n.83, bf16[384,2048]{1,0:T(8,128)(2,1)S(1)} %get-tuple-element.8, bf16[384,2048]{1,0:T(8,128)(2,1)S(1)} %collective-permute-done.6, bf16[384,1024]{1,0:T(8,128)(2,1)} %collective-permute-done.4, bf16[384,1024]{1,0:T(8,128)(2,1)S(1)} %bitcast.123), kind=kOutput, calls=%fused_computation.25 | convolution fusion | flops 810549248 | bytes 5767172 | tf_op jit(solution)/shard_map/weight_grad/dot_general | solution.py:68
  86.3 3.1 %convolution_convert_fusion = bf16[512,1024]{1,0:T(8,128)(2,1)} fusion(s32[]{:T(128)S(6)} %select_n.85, bf16[384,2048]{1,0:T(8,128)(2,1)S(1)} %get-tuple-element.8, bf16[384,2048]{1,0:T(8,128)(2,1)S(1)} %collective-permute-done.6, bf16[384,1024]{1,0:T(8,128)(2,1)} %collective-permute-done.4, bf16[384,1024]{1,0:T(8,128)(2,1)S(1)} %bitcast.124), kind=kOutput, calls=%fused_computation.24 | convolution fusion | flops 810549248 | bytes 5767172 | tf_op jit(solution)/shard_map/weight_grad/dot_general | solution.py:68
  91.0 3.5 %fusion.15 = f32[512,1024]{1,0:T(8,128)} fusion(s32[]{:T(128)S(6)} %select_n.79, bf16[384,2048]{1,0:T(8,128)(2,1)S(1)} %get-tuple-element.8, bf16[384,2048]{1,0:T(8,128)(2,1)S(1)} %collective-permute-done.6, bf16[384,1024]{1,0:T(8,128)(2,1)} %collective-permute-done.4, bf16[384,1024]{1,0:T(8,128)(2,1)S(1)} %bitcast.125), kind=kOutput, calls=%fused_computation.46 | convolution fusion | flops 810024960 | bytes 6815748 | tf_op jit(solution)/shard_map/weight_grad/dot_general | solution.py:68
  98.6 2.0 %fusion.1 = bf16[4,384,512]{2,1,0:T(8,128)(2,1)S(1)} fusion(s32[]{:T(128)S(6)} %select_n.74, bf16[4,384,512]{2,1,0:T(8,128)(2,1)} %collective-permute-done.5), kind=kLoop, calls=%fused_computation.17 | loop fusion | flops 786432 | bytes 3145732 | tf_op jit(solution)/shard_map/assemble/concatenate | solution.py:78
  100.8 2.3 %collective-permute-done.3 = bf16[4,384,512]{2,1,0:T(8,128)(2,1)} collective-permute-done((bf16[4,384,512]{2,1,0:T(8,128)(2,1)}, bf16[4,384,512]{2,1,0:T(8,128)(2,1)}, u32[]{:S(2)}, u32[]{:S(2)}) %collective-permute-start.3) | collective-permute-done | bytes 1572896 | tf_op jit(solution)/shard_map/input_grad/ppermute | solution.py:23
  103.1 2.0 %fusion.2 = bf16[4,384,512]{2,1,0:T(8,128)(2,1)S(1)} fusion(s32[]{:T(128)S(6)} %select_n.74, bf16[4,384,512]{2,1,0:T(8,128)(2,1)} %collective-permute-done.3), kind=kLoop, calls=%fused_computation.18 | loop fusion | flops 786432 | bytes 3145732 | tf_op jit(solution)/shard_map/assemble/concatenate | solution.py:78
  105.7 22.5 %collective-permute-done.8 = bf16[512,1024]{1,0:T(8,128)(2,1)} collective-permute-done((bf16[512,1024]{1,0:T(8,128)(2,1)}, bf16[512,1024]{1,0:T(8,128)(2,1)}, u32[]{:S(2)}, u32[]{:S(2)}) %collective-permute-start.8) | collective-permute-done | bytes 1048608 | tf_op jit(solution)/shard_map/weight_grad/ppermute | solution.py:23
  128.9 3.6 %fusion.11 = bf16[1,1,512,1024]{3,2,1,0:T(8,128)(2,1)} fusion(bf16[512,1024]{1,0:T(8,128)(2,1)} %collective-permute-done.9, bf16[512,1024]{1,0:T(8,128)(2,1)} %collective-permute-done.8, f32[512,1024]{1,0:T(8,128)S(1)} %copy-done.1, bf16[512,1024]{1,0:T(8,128)(2,1)} %collective-permute-done.7), kind=kLoop, calls=%fused_computation.43 | loop fusion | flops 3670016 | bytes 6291456 | tf_op jit(solution)/shard_map/broadcast_in_dim | solution.py:83
  132.5 2.0 %broadcast_select_fusion = bf16[1,1,384,4096]{3,2,1,0:T(8,128)(2,1)} fusion(bf16[1,1,384,4096]{3,2,1,0:T(8,128)(2,1)S(1)} %fusion.36, bf16[1,1,384,4096]{3,2,1,0:T(8,128)(2,1)S(1)} %get-tuple-element.9, pred[]{:T(512)S(6)} %eq.11), kind=kLoop, calls=%fused_computation.12 | loop fusion | flops 1572864 | bytes 9437185 | tf_op jit(solution)/shard_map/assemble/jit(_where)/select_n | solution.py:82
  134.5 4.4 %all-gather.2.cloned.1.call-done = bf16[512,1024]{1,0:T(8,128)(2,1)} async-done(((bf16[64,1024]{1,0:T(8,128)(2,1)}), bf16[512,1024]{1,0:T(8,128)(2,1)}) %all-gather.2.cloned.1.call-update) | async-done | bytes 1048592 | tf_op jit(solution)/shard_map/outer/all_gather | solution.py:51
  138.9 2.3 %copy.28 = bf16[1,512,1024]{2,1,0:T(8,128)(2,1)} copy(bf16[1,512,1024]{2,1,0:T(8,128)(2,1)} %bitcast.126) | data formatting | bytes 2097152
  (46 shorter events, 13.8 us)
Async XLA Ops:
  7.2 37.1 %collective-permute-start.2 = (bf16[512,1024]{1,0:T(8,128)(2,1)}, bf16[512,1024]{1,0:T(8,128)(2,1)}, u32[]{:S(2)}, u32[]{:S(2)}) collective-permute-start(bf16[512,1024]{1,0:T(8,128)(2,1)} %bitcast.128), channel_id=1, source_target_pairs={{1,5},{2,6},{3,7},{5,9},{6,10},{7,11},{9,13},{10,14},{11,15},{13,1... | collective-permute-start | bytes 3145736 | tf_op jit(solution)/shard_map/gather_weight/ppermute | solution.py:23
  10.7 35.7 %collective-permute-start = (bf16[512,1024]{1,0:T(8,128)(2,1)}, bf16[512,1024]{1,0:T(8,128)(2,1)}, u32[]{:S(2)}, u32[]{:S(2)}) collective-permute-start(bf16[512,1024]{1,0:T(8,128)(2,1)} %bitcast.129), channel_id=1, source_target_pairs={{1,13},{2,14},{3,15},{5,1},{6,2},{7,3},{9,5},{10,6},{11,7},{13,9},... | collective-permute-start | bytes 3145736 | tf_op jit(solution)/shard_map/gather_weight/ppermute | solution.py:23
  14.2 45.0 %collective-permute-start.1 = (bf16[512,1024]{1,0:T(8,128)(2,1)}, bf16[512,1024]{1,0:T(8,128)(2,1)}, u32[]{:S(2)}, u32[]{:S(2)}) collective-permute-start(bf16[512,1024]{1,0:T(8,128)(2,1)} %bitcast.130), channel_id=1, source_target_pairs={{1,9},{2,10},{3,11},{5,13},{6,14},{7,15},{9,1},{10,2},{11,3},{13,5... | collective-permute-start | bytes 3145736 | tf_op jit(solution)/shard_map/gather_weight/ppermute | solution.py:23
  18.1 24.4 %collective-permute-start.4 = (bf16[384,1024]{1,0:T(8,128)(2,1)}, bf16[384,1024]{1,0:T(8,128)(2,1)}, u32[]{:S(2)}, u32[]{:S(2)}) collective-permute-start(bf16[384,1024]{1,0:T(8,128)(2,1)} %bitcast.121), channel_id=1, source_target_pairs={{0,16},{1,17},{2,18},{3,19},{4,20},{5,21},{6,22},{7,23},{8,24},{9,... | collective-permute-start | bytes 2359304 | tf_op jit(solution)/shard_map/pair_swap/ppermute | solution.py:23
  19.4 4.3 %copy-start.4 = (s32[1,1,512,8]{2,3,1,0:T(8,128)S(1)}, s32[1,1,512,8]{2,3,1,0:T(8,128)}, u32[]{:S(2)}) copy-start(s32[1,1,512,8]{2,3,1,0:T(8,128)} %param.11) | copy-start | bytes 49156
  22.9 50.5 %collective-permute-start.6 = (bf16[384,2048]{1,0:T(8,128)(2,1)}, bf16[384,2048]{1,0:T(8,128)(2,1)S(1)}, u32[]{:S(2)}, u32[]{:S(2)}) collective-permute-start(bf16[384,2048]{1,0:T(8,128)(2,1)} %get-tuple-element.7), channel_id=1, source_target_pairs={{0,16},{1,17},{2,18},{3,19},{4,20},{5,21},{6,22},{7,23},{8,24},{9,... | collective-permute-start | bytes 4718600 | tf_op jit(solution)/shard_map/pair_swap/ppermute | solution.py:23
  31.7 62.8 %all-to-all-start = ((bf16[8,64,1024]{2,1,0:T(8,128)(2,1)}), bf16[8,64,1024]{2,1,0:T(8,128)(2,1)}, u32[]{:S(2)}, u32[]{:S(2)}) async-start(bf16[8,64,1024]{2,1,0:T(8,128)(2,1)} %fusion), calls=%async_computation | async-start | bytes 2097152 | tf_op jit(solution)/shard_map/outer/all_to_all | solution.py:47
  40.2 98.8 %all-gather.2.cloned.1.call-start = ((), (), s32[]{:S(2)}) async-start(), calls=%async_computation.1 | async-start | bytes 1179648 | tf_op jit(solution)/shard_map/outer/all_gather | solution.py:51
  40.3 2.2 %copy-start.5 = (bf16[1,1,512,1024]{3,2,1,0:T(8,128)(2,1)S(1)}, bf16[1,1,512,1024]{3,2,1,0:T(8,128)(2,1)}, u32[]{:S(2)}) copy-start(bf16[1,1,512,1024]{3,2,1,0:T(8,128)(2,1)} %param.9) | copy-start | bytes 3145732
  61.3 3.3 %copy-start = (bf16[1,1,384,1024]{3,2,1,0:T(8,128)(2,1)S(1)}, bf16[1,1,384,1024]{3,2,1,0:T(8,128)(2,1)}, u32[]{:S(2)}) copy-start(bf16[1,1,384,1024]{3,2,1,0:T(8,128)(2,1)} %param.8) | copy-start | bytes 2359300
  62.7 35.9 %collective-permute-start.5 = (bf16[4,384,512]{2,1,0:T(8,128)(2,1)}, bf16[4,384,512]{2,1,0:T(8,128)(2,1)}, u32[]{:S(2)}, u32[]{:S(2)}) collective-permute-start(bf16[4,384,512]{2,1,0:T(8,128)(2,1)} %pad_maximum_fusion.1), channel_id=1, source_target_pairs={{1,16},{2,17},{3,18},{5,20},{6,21},{7,22},{9,24},{10,25},{11,26},{... | collective-permute-start | bytes 4718600 | tf_op jit(solution)/shard_map/input_grad/ppermute | solution.py:23
  71.5 31.7 %collective-permute-start.3 = (bf16[4,384,512]{2,1,0:T(8,128)(2,1)}, bf16[4,384,512]{2,1,0:T(8,128)(2,1)}, u32[]{:S(2)}, u32[]{:S(2)}) collective-permute-start(bf16[4,384,512]{2,1,0:T(8,128)(2,1)} %pad_maximum_fusion), channel_id=1, source_target_pairs={{1,0},{2,1},{3,2},{5,4},{6,5},{7,6},{9,8},{10,9},{11,10},{13,12},{... | collective-permute-start | bytes 4718600 | tf_op jit(solution)/shard_map/input_grad/ppermute | solution.py:23
  76.6 29.1 %collective-permute-start.7 = (bf16[512,1024]{1,0:T(8,128)(2,1)}, bf16[512,1024]{1,0:T(8,128)(2,1)}, u32[]{:S(2)}, u32[]{:S(2)}) collective-permute-start(bf16[512,1024]{1,0:T(8,128)(2,1)} %convolution_convert_fusion.2), channel_id=1, source_target_pairs={{0,8},{1,9},{2,10},{3,11},{4,12},{5,13},{6,14},{7,15},{8,0},{9,1},... | collective-permute-start | bytes 3145736 | tf_op jit(solution)/shard_map/weight_grad/ppermute | solution.py:23
  84.6 43.6 %collective-permute-start.8 = (bf16[512,1024]{1,0:T(8,128)(2,1)}, bf16[512,1024]{1,0:T(8,128)(2,1)}, u32[]{:S(2)}, u32[]{:S(2)}) collective-permute-start(bf16[512,1024]{1,0:T(8,128)(2,1)} %convolution_convert_fusion.1), channel_id=1, source_target_pairs={{0,4},{1,5},{2,6},{3,7},{4,8},{5,9},{6,10},{7,11},{8,12},{9,13},{1... | collective-permute-start | bytes 3145736 | tf_op jit(solution)/shard_map/weight_grad/ppermute | solution.py:23
  89.4 6.5 %copy-start.2 = (f32[1,64,1024]{2,1,0:T(8,128)S(1)}, f32[1,64,1024]{2,1,0:T(8,128)}, u32[]{:S(2)}) copy-start(f32[1,64,1024]{2,1,0:T(8,128)} %param.13) | copy-start | bytes 786436
  89.4 39.4 %collective-permute-start.9 = (bf16[512,1024]{1,0:T(8,128)(2,1)}, bf16[512,1024]{1,0:T(8,128)(2,1)}, u32[]{:S(2)}, u32[]{:S(2)}) collective-permute-start(bf16[512,1024]{1,0:T(8,128)(2,1)} %convolution_convert_fusion), channel_id=1, source_target_pairs={{0,12},{1,13},{2,14},{3,15},{4,0},{5,1},{6,2},{7,3},{8,4},{9,5},{1... | collective-permute-start | bytes 3145736 | tf_op jit(solution)/shard_map/weight_grad/ppermute | solution.py:23
  94.5 3.2 %copy-start.3 = (f32[1,64,1024]{2,1,0:T(8,128)S(1)}, f32[1,64,1024]{2,1,0:T(8,128)}, u32[]{:S(2)}) copy-start(f32[1,64,1024]{2,1,0:T(8,128)} %param.12) | copy-start | bytes 786436
  105.4 23.5 %copy-start.1 = (f32[512,1024]{1,0:T(8,128)S(1)}, f32[512,1024]{1,0:T(8,128)}, u32[]{:S(2)}) copy-start(f32[512,1024]{1,0:T(8,128)} %fusion.15) | copy-start | bytes 6291460
Sparse Core Ops, SparseCore 0:
  97.8 41.1 all-gather.1

commit v2 on v1

v2 whole, which is shorter than its diff:
```python
import jax
import jax.numpy as jnp
from jax import lax
from jax.experimental import pallas as pl
from jax.experimental.pallas import tpu as pltpu
from jax.sharding import PartitionSpec as P

NX, NY = 2, 4
BF16, F32 = jnp.bfloat16, jnp.float32
PARAMS = pltpu.CompilerParams(vmem_limit_bytes=48 * 1024 * 1024)


def call(kernel, name, grid, in_specs, out_specs, out_shape, aliases=None, after=()):
    inputs, count = len(in_specs), len(after)

    def with_after(pos, *refs):
        kernel(pos, *refs[:inputs], *refs[inputs + count:])

    run = pl.pallas_call(
        with_after,
        grid_spec=pltpu.PrefetchScalarGridSpec(
            num_scalar_prefetch=1, grid=grid, in_specs=list(in_specs) + [pl.BlockSpec(memory_space=pl.ANY)] * count,
            out_specs=out_specs),
        out_shape=out_shape,
        input_output_aliases=aliases or {},
        compiler_params=PARAMS,
        cost_estimate=pl.CostEstimate(flops=1, bytes_accessed=1, transcendentals=0),
        name=name,
    )
    return lambda *operands: run(*operands, *after)


def block_of(pos, r):
    return lax.rem(pos[1] + r, NY)


def scaled(codes_ref, exps_ref, out_ref):
    scales = jnp.exp2(exps_ref[...].astype(F32))
    blocks = scales.shape[1]
    wide = codes_ref.shape[1] // blocks
    for b in range(blocks):
        cols = slice(b * wide, (b + 1) * wide)
        out_ref[:, cols] = (codes_ref[:, cols].astype(F32) * scales[:, b:b + 1]).astype(BF16)


def delta_kernel(pos, codes_keep, codes_send, exps_keep, exps_send, keep_ref, send_ref):
    scaled(codes_keep, exps_keep, keep_ref)
    scaled(codes_send, exps_send, send_ref)


def add_kernel(pos, keep, arrived, out_ref):
    out_ref[...] = (keep[...].astype(F32) + arrived[...].astype(F32)).astype(BF16)


def input_grad(c_ref, c_o_ref, w_ref):
    both = jnp.concatenate([c_ref[...], c_o_ref[...]], 0)
    out = lax.dot_general(
        both, w_ref[...], (((1,), (1,)), ((), ())), preferred_element_type=F32).astype(BF16)
    return out[:c_ref.shape[0]], out[c_ref.shape[0]:]


def input_grad_kernel(pos, c_ref, c_o_ref, *refs):
    *w_refs, own_ref, other_ref = refs
    for i, w_ref in enumerate(w_refs):
        @pl.when(pl.program_id(0) == i)
        def _():
            own_ref[...], other_ref[...] = input_grad(c_ref, c_o_ref, w_ref)


def far_input_grad_kernel(pos, c_ref, c_o_ref, up_ref, down_ref, own_ref, other_ref):
    half = up_ref.shape[0]
    own_ref[:, :half], other_ref[:, :half] = input_grad(c_ref, c_o_ref, up_ref)
    own_ref[:, half:], other_ref[:, half:] = input_grad(c_ref, c_o_ref, down_ref)


def partial_grad(a_ref, a_o_ref, c_ref, c_o_ref):
    dims = (((0,), (0,)), ((), ()))
    return lax.dot_general(a_ref[...], c_ref[...], dims, preferred_element_type=F32) + lax.dot_general(
        a_o_ref[...], c_o_ref[...], dims, preferred_element_type=F32)


def far_grad_kernel(pos, a_ref, a_o_ref, c_ref, c_o_ref, w_up, w_down, up_ref, down_ref):
    total = partial_grad(a_ref, a_o_ref, c_ref, c_o_ref).astype(BF16)
    half = total.shape[0] // 2
    up_ref[:half] = total[:half]
    up_ref[half:] = w_up[...]
    down_ref[:half] = total[half:]
    down_ref[half:] = w_down[...]


def near_grad_kernel(upper, pos, a_ref, a_o_ref, c_ref, c_o_ref, arrived, out_ref):
    total = partial_grad(a_ref, a_o_ref, c_ref, c_o_ref)
    half = arrived.shape[0]
    first, second = total[:half], total[half:]
    if upper:
        first = first + arrived[...].astype(F32)
    else:
        second = second + arrived[...].astype(F32)
    out_ref[:half] = first.astype(BF16)
    out_ref[half:] = second.astype(BF16)


def last_grad_kernel(pos, a_ref, a_o_ref, c_ref, c_o_ref, p1, p3, out_ref):
    total = partial_grad(a_ref, a_o_ref, c_ref, c_o_ref)
    total = total + p1[...].astype(F32) + p3[...].astype(F32)
    out_ref[...] = total.astype(BF16)


def outer_kernel(pos, d_ref, mom_ref, mas_ref, mom_out, mas_out, sync_out):
    count = d_ref.shape[0]
    total = d_ref[0].astype(F32)
    for i in range(1, count):
        total = total + d_ref[i].astype(F32)
    mean = total / (2 * count)
    mom = 0.9 * mom_ref[...] + mean
    mas = mas_ref[...] - 0.7 * (mean + 0.9 * mom)
    mom_out[...] = mom
    mas_out[...] = mas
    synced = mas.astype(BF16)
    for i in range(sync_out.shape[0]):
        sync_out[i] = synced


def place_kernel(pos, most, rest, *refs):
    step = pl.program_id(0)
    out_ref = refs[-1]

    @pl.when(step < NY - 1)
    def _():
        out_ref[...] = most[...]

    @pl.when(step == NY - 1)
    def _():
        out_ref[...] = rest[...]


def copy_kernel(pos, part_ref, *refs):
    refs[-1][...] = part_ref[...]


def solution(mesh):
    sections = mesh.shape["section"]
    replicas = mesh.shape["replica"]

    def moved(value, to, first=0):
        pairs = []
        for x in range(NX):
            for y in range(NY):
                for s in range(first, sections):
                    tx, ty, ts = to(x, y, s)
                    if 0 <= ts < sections:
                        source = (x * NY + y) * sections + s
                        target = (tx % NX * NY + ty % NY) * sections + ts
                        pairs.append((source, target))
        return lax.ppermute(value, ("dp", "section"), pairs)

    def body(act, cot, w, codes, exps, mom, mas):
        act, cot, w, codes, exps, mom, mas = (
            act[0, 0], cot[0, 0], w[0, 0], codes[0, 0], exps[0, 0], mom[0], mas[0])
        rows, width = w.shape
        tok = act.shape[0]
        dp = lax.axis_index("dp")
        pos = jnp.stack([dp // NY, dp % NY, lax.axis_index("replica") % 2]).astype(jnp.int32)
        whole = lambda shape: pl.BlockSpec(shape, lambda *_: (0,) * len(shape))
        share, half = rows // replicas, rows // 2
        up = lambda x, y, s: (x, y + 1, s)
        down = lambda x, y, s: (x, y - 1, s)
        swap = lambda x, y, s: (x + 1, y, s)

        def swapped_blocks(rs, after):
            number, count = rs
            at = lambda i, pos: (0, (1 - pos[0]) * NY + block_of(pos, number(i)))
            send = call(
                copy_kernel, "split", (count,), [pl.BlockSpec((tok, rows), at)],
                pl.BlockSpec((tok, rows), lambda i, pos: (0, i)),
                jax.ShapeDtypeStruct((tok, count * rows), BF16), after=after,
            )(pos, act)
            return send, moved(send, swap)

        def part_rows(n, m):
            return pl.BlockSpec((n, m), lambda i, pos: (i, 0))

        def part_of(shape, i, j):
            return pl.BlockSpec(shape, lambda *_: (i, j))

        def blocks(r, part):
            return [pl.BlockSpec((tok, rows), lambda _, pos: (0, pos[0] * NY + block_of(pos, r))),
                    part_of((tok, rows), 0, part), whole((tok, width)), whole((tok, width))]

        def near(r, part, arrived, after):
            part = call(
                lambda *refs: near_grad_kernel(r == 1, *refs), "near_grad", (1,),
                blocks(r, part) + [part_of((half, width), 0, 0)], whole((rows, width)),
                jax.ShapeDtypeStruct((rows, width), BF16), after=after,
            )(pos, act, act_o, cot, cot_o, arrived)
            return part, moved(part, up if r == 1 else down)

        def place(most, rest, flip, after, base=None):
            number = lambda i: i + i // 2 - i // 3 * 2
            at = lambda i, pos: (0, (1 - pos[0] if flip else pos[0]) * NY + block_of(pos, number(i)))
            return call(
                place_kernel, "place", (NY,),
                [pl.BlockSpec((tok, rows), lambda i, pos: (0, jnp.minimum(i, NY - 2))), whole((tok, rows))]
                + ([pl.BlockSpec(memory_space=pl.ANY)] if base is not None else []),
                pl.BlockSpec((tok, rows), at), jax.ShapeDtypeStruct(act.shape, BF16),
                {3: 0} if base is not None else None, after=after,
            )(pos, most, rest, *([base] if base is not None else []))

        with jax.named_scope("pair_swap"):
            send, act_2 = swapped_blocks((lambda i: 2, 1), [])
            cot_o = moved(cot, swap)
        with jax.named_scope("gather_weight"):
            w_3 = moved(w, up)
            w_1 = moved(w, down)
        with jax.named_scope("delta"):
            row = lambda n, other: pl.BlockSpec(
                (share, n), lambda i, pos: (2 * i + (1 - pos[2] if other else pos[2]), 0))
            out = pl.BlockSpec((share, width), lambda i, pos: (i, 0))
            n_exp = exps.shape[1]
            keep, send = call(
                delta_kernel, "delta", (replicas // 2,),
                [row(width, False), row(width, True), row(n_exp, False), row(n_exp, True)],
                [out, out], [jax.ShapeDtypeStruct((rows // 2, width), BF16)] * 2, after=[send],
            )(pos, codes, codes, exps, exps)
            arrived = lax.ppermute(send, "replica", [(i, i ^ 1) for i in range(replicas)])
            pair_sum = call(
                add_kernel, "add", (2,), [part_rows(half // 2, width)] * 2, part_rows(half // 2, width),
                jax.ShapeDtypeStruct((half, width), BF16), after=[w_3, w_1, cot_o],
            )(pos, keep, arrived)
            deltas = lax.all_to_all(
                pair_sum.reshape(replicas // 2, share, width), "replica", 0, 0,
                axis_index_groups=[list(range(k, replicas, 2)) for k in range(2)])
        with jax.named_scope("far"):
            far_up, far_down = call(
                far_grad_kernel, "far_grad", (1,),
                blocks(2, 0) + [part_of((half, width), 0, 0), part_of((half, width), 1, 0)],
                [whole((rows, width))] * 2, [jax.ShapeDtypeStruct((rows, width), BF16)] * 2, after=[pair_sum],
            )(pos, act, act_2, cot, cot_o, w_3, w_1)
            up_o = moved(far_up, up)
            down_o = moved(far_down, down)
        with jax.named_scope("pair_swap"):
            send, act_o = swapped_blocks((lambda i: 2 * i + 1 - 5 * (i // 2), 3), [far_up])
        with jax.named_scope("input_grad"):
            shift = lambda x, y, s: (x, y, s - 1)
            flip = lambda x, y, s: (x + 1, y, s - 1)
            out = pl.BlockSpec((tok, rows), lambda i, pos: (0, i))
            own, other = call(
                input_grad_kernel, "input_grad", (NY - 1,),
                [whole((tok, width))] * 2 + [whole((rows, width))] * 3, [out, out],
                [jax.ShapeDtypeStruct((tok, (NY - 1) * rows), BF16)] * 2, after=[send],
            )(pos, cot, cot_o, w, w_1, w_3)
            sent_other, sent_own = moved(other, flip, 1), moved(own, shift, 1)
        with jax.named_scope("outer"):
            cols = width // 2
            wide = pl.BlockSpec((replicas, share, cols), lambda i, pos: (0, 0, i))
            some = pl.BlockSpec((replicas // 2, share, cols), lambda i, pos: (0, 0, i))
            thin = pl.BlockSpec((share, cols), lambda i, pos: (0, i))
            mom_new, mas_new, to_sync = call(
                outer_kernel, "outer", (2,), [some, thin, thin], [thin, thin, wide],
                [jax.ShapeDtypeStruct(mom.shape, F32)] * 2
                + [jax.ShapeDtypeStruct((replicas, share, width), BF16)], after=[own],
            )(pos, deltas, mom, mas)
            synced = lax.all_to_all(to_sync, "replica", 0, 0).reshape(rows, width)
        with jax.named_scope("weight_grad"):
            part, near_1 = near(1, 0, up_o, [to_sync])
            part, near_3 = near(3, 1, down_o, [part])
        with jax.named_scope("input_grad"):
            own, other = call(
                far_input_grad_kernel, "far_input_grad", (1,),
                [whole((tok, width))] * 2 + [part_of((half, width), 1, 0)] * 2, [whole((tok, rows))] * 2,
                [jax.ShapeDtypeStruct((tok, rows), BF16)] * 2, after=[part],
            )(pos, cot, cot_o, up_o, down_o)
            sent_other_2, sent_own_2 = moved(other, flip, 1), moved(own, shift, 1)
        with jax.named_scope("assemble"):
            sent = place(sent_own, sent_own_2, False, [own])
            sent = place(sent_other, sent_other_2, True, [], sent)
        with jax.named_scope("weight_grad"):
            grad = call(
                last_grad_kernel, "last_grad", (1,), blocks(0, 2) + [whole((rows, width))] * 2,
                whole((rows, width)), jax.ShapeDtypeStruct((rows, width), BF16), after=[sent],
            )(pos, act, act_o, cot, cot_o, near_1, near_3)
        return (sent[None, None], grad[None, None], mom_new[None], mas_new[None], synced[None])

    placed = (
        P("replica", "section", "dp", None),
        P("replica", "section", "dp", None),
        P("replica", "section", "dp", None),
        P("replica", "section", "dp", None),
        P("replica", "section", "dp", None),
        P("section", ("dp", "replica"), None),
        P("section", ("dp", "replica"), None),
    )
    return jax.shard_map(
        body,
        mesh=mesh,
        in_specs=placed,
        out_specs=(
            P("replica", "section", "dp", None),
            P("replica", "section", "dp", None),
            P("section", ("dp", "replica"), None),
            P("section", ("dp", "replica"), None),
            P("section", "dp", None),
        ),
        check_vma=False,
    )
```

time: 149 us -> 122 us (0.82)
  the two profiles are of different devices: /device:TPU:4 before, /device:TPU:1 now
where the time goes in v2:
time: 122 us; the launch traced here: 121 us
  starting transfers between devices  44 us (36%)
  Pallas kernels  33.9 us (28%)
  waiting for transfers between devices  29.7 us (24%)
  local copies, waits for them, and re-layouts  13 us (11%)
    pallas_call x13, Pallas kernels, call(): return lambda *operands: run(*operands, *after)  33.9 us
    ppermute x13, starting transfers between devices, moved(): return lax.ppermute(value, ('dp', 'section'), pairs)  26.6 us
    ppermute x13, waiting for transfers between devices, moved(): return lax.ppermute(value, ('dp', 'section'), pairs)  19.5 us
    unnamed x42, local copies, waits for them, and re-layouts  13 us
    ppermute x1, waiting for transfers between devices, body(): lax.ppermute(send, 'replica', [(i, i ^ 1) for i in range(replicas)])  10.3 us
    all_to_all x1, starting transfers between devices, body(): lax.all_to_all(pair_sum.reshape(replicas // 2, share, width), 'replica',...  8.88 us
    all_to_all x1, starting transfers between devices, body(): synced = lax.all_to_all(to_sync, 'replica', 0, 0).reshape(rows, width)  6.77 us
  transfers between devices with their start and end apart: 16, of which 7 were waited for; matrix products, arithmetic and copies ran while one was open for 1% of the time, Pallas kernels for 28%

profile of v2, /device:TPU:1, one launch (start us, length us, event | category | flops | bytes accessed | tf_op | source)
XLA Modules:
  0.0 121.5 jit_solution(18285062483460737973)
XLA Ops:
  0.6 2.2 %collective-permute-start.2 = (bf16[512,1024]{1,0:T(8,128)(2,1)}, bf16[512,1024]{1,0:T(8,128)(2,1)S(1)}, u32[]{:S(2)}, u32[]{:S(2)}) collective-permute-start(bf16[512,1024]{1,0:T(8,128)(2,1)} %bitcast.33), channel_id=1, source_target_pairs={{0,4},{1,5},{2,6},{3,7},{4,8},{5,9},{6,10},{7,11},{8,12},{9,13},{1... | collective-permute-start | bytes 3145736 | tf_op jit(solution)/shard_map/gather_weight/ppermute | solution.py:155
  2.8 1.5 %collective-permute-start.1 = (bf16[512,1024]{1,0:T(8,128)(2,1)}, bf16[512,1024]{1,0:T(8,128)(2,1)S(1)}, u32[]{:S(2)}, u32[]{:S(2)}) collective-permute-start(bf16[512,1024]{1,0:T(8,128)(2,1)} %bitcast.34), channel_id=1, source_target_pairs={{0,12},{1,13},{2,14},{3,15},{4,0},{5,1},{6,2},{7,3},{8,4},{9,5},{1... | collective-permute-start | bytes 3145736 | tf_op jit(solution)/shard_map/gather_weight/ppermute | solution.py:155
  5.7 1.9 %copy-done = bf16[1,1,384,4096]{3,2,1,0:T(8,128)(2,1)S(1)} copy-done((bf16[1,1,384,4096]{3,2,1,0:T(8,128)(2,1)S(1)}, bf16[1,1,384,4096]{3,2,1,0:T(8,128)(2,1)}, u32[]{:S(2)}) %copy-start) | copy-done | bytes 3145752
  10.2 1.5 %delta.1 = (bf16[256,1024]{1,0:T(8,128)(2,1)S(1)}, bf16[256,1024]{1,0:T(8,128)(2,1)S(1)}) custom-call(s32[3]{0:T(128)S(1)} %pad_add_fusion.pos, bf16[512,1024]{1,0:T(8,128)(2,1)S(1)} %bitcast.29, bf16[512,1024]{1,0:T(8,128)(2,1)S(1)} %bitcast.30, s32[512,8]{1,0:T(8,128)S(1)} %bitcast.31, s32[512,8]{1,0:T(8,128)S(1)} %bitcast.32, ...), custom_call_target="tpu_custom_call" | custom-call | flops 1 | bytes 1 | tf_op jit(solution)/shard_map/delta/delta/pallas_call | solution.py:30
  11.7 1.7 %collective-permute-start.4 = (bf16[256,1024]{1,0:T(8,128)(2,1)S(1)}, bf16[256,1024]{1,0:T(8,128)(2,1)S(1)}, u32[]{:S(2)}, u32[]{:S(2)}) collective-permute-start(bf16[256,1024]{1,0:T(8,128)(2,1)S(1)} %get-tuple-element.17), channel_id=1, source_target_pairs={{0,32},{32,0},{64,96},{96,64},{128,160},{160,128},{192,224},{224,1... | collective-permute-start | bytes 1572872 | tf_op jit(solution)/shard_map/delta/ppermute | solution.py:225
  13.7 10.3 %collective-permute-done.4.refs_1_ = bf16[256,1024]{1,0:T(8,128)(2,1)S(1)} collective-permute-done((bf16[256,1024]{1,0:T(8,128)(2,1)S(1)}, bf16[256,1024]{1,0:T(8,128)(2,1)S(1)}, u32[]{:S(2)}, u32[]{:S(2)}) %collective-permute-start.4) | collective-permute-done | bytes 524320 | tf_op jit(solution)/shard_map/delta/ppermute | solution.py:225
  24.0 1.4 %collective-permute-done.2.refs_2_.refs_4_ = bf16[512,1024]{1,0:T(8,128)(2,1)S(1)} collective-permute-done((bf16[512,1024]{1,0:T(8,128)(2,1)}, bf16[512,1024]{1,0:T(8,128)(2,1)S(1)}, u32[]{:S(2)}, u32[]{:S(2)}) %collective-permute-start.2) | collective-permute-done | bytes 1048608 | tf_op jit(solution)/shard_map/gather_weight/ppermute | solution.py:155
  26.5 1.4 %add.15.refs_6_ = bf16[256,1024]{1,0:T(8,128)(2,1)} custom-call(s32[3]{0:T(128)S(1)} %pad_add_fusion.pos, bf16[256,1024]{1,0:T(8,128)(2,1)S(1)} %get-tuple-element.16.refs_0_, bf16[256,1024]{1,0:T(8,128)(2,1)S(1)} %collective-permute-done.4.refs_1_, bf16[512,1024]{1,0:T(8,128)(2,1)S(1)} %collective-permute-done.2.refs_2_.refs_4_, ...), custom_call_target="tpu_custom_call" | custom-call | flops 1 | bytes 1 | tf_op jit(solution)/shard_map/delta/add/pallas_call | solution.py:30
  27.9 8.9 %all-to-all-start = ((bf16[4,64,1024]{2,1,0:T(8,128)(2,1)}), bf16[4,64,1024]{2,1,0:T(8,128)(2,1)S(1)}, u32[]{:S(2)}, u32[]{:S(2)}) async-start(bf16[4,64,1024]{2,1,0:T(8,128)(2,1)} %bitcast.8), calls=%async_computation | async-start | bytes 1048576 | tf_op jit(solution)/shard_map/delta/all_to_all | solution.py:230
  39.1 1.2 %copy-done.10 = bf16[512,1024]{1,0:T(8,128)(2,1)S(1)} copy-done((bf16[512,1024]{1,0:T(8,128)(2,1)S(1)}, bf16[512,1024]{1,0:T(8,128)(2,1)}, u32[]{:S(2)}) %copy-start.10) | copy-done | bytes 1048600
  40.3 4.6 %far_grad.1 = (bf16[512,1024]{1,0:T(8,128)(2,1)}, bf16[512,1024]{1,0:T(8,128)(2,1)}) custom-call(s32[3]{0:T(128)S(1)} %pad_add_fusion.pos, bf16[384,4096]{1,0:T(8,128)(2,1)} %bitcast.16, bf16[384,512]{1,0:T(8,128)(2,1)} %collective-permute-done.3.refs_1_, bf16[384,1024]{1,0:T(8,128)(2,1)S(1)} %bitcast.23, bf16[384,1024]{1,0:T(8,128)(2,1)S(1)} %copy-done.3, ...), custom_call_target="tpu_custom_call" | custom-call | flops 1 | bytes 1 | tf_op jit(solution)/shard_map/far/far_grad/pallas_call | solution.py:30
  45.0 2.2 %split.3.refs_5_ = bf16[384,1536]{1,0:T(8,128)(2,1)} custom-call(s32[3]{0:T(128)S(1)} %pad_add_fusion.pos, bf16[384,4096]{1,0:T(8,128)(2,1)S(1)} %bitcast.21, bf16[512,1024]{1,0:T(8,128)(2,1)} %get-tuple-element.18.refs_1_), custom_call_target="tpu_custom_call" | custom-call | flops 1 | bytes 1 | tf_op jit(solution)/shard_map/pair_swap/split/pallas_call | solution.py:30
  49.4 1.7 %collective-permute-start.7 = (bf16[512,1024]{1,0:T(8,128)(2,1)}, bf16[512,1024]{1,0:T(8,128)(2,1)}, u32[]{:S(2)}, u32[]{:S(2)}) collective-permute-start(bf16[512,1024]{1,0:T(8,128)(2,1)} %get-tuple-element.20), channel_id=1, source_target_pairs={{0,12},{1,13},{2,14},{3,15},{4,0},{5,1},{6,2},{7,3},{8,4},{9,5},{1... | collective-permute-start | bytes 3145736 | tf_op jit(solution)/shard_map/far/ppermute | solution.py:155
  51.1 4.6 %input_grad.1 = (bf16[384,1536]{1,0:T(8,128)(2,1)S(1)}, bf16[384,1536]{1,0:T(8,128)(2,1)}) custom-call(s32[3]{0:T(128)S(1)} %pad_add_fusion.pos, bf16[384,1024]{1,0:T(8,128)(2,1)S(1)} %bitcast.24, bf16[384,1024]{1,0:T(8,128)(2,1)S(1)} %copy-done.4, bf16[512,1024]{1,0:T(8,128)(2,1)S(1)} %bitcast.35, bf16[512,1024]{1,0:T(8,128)(2,1)S(1)} %copy-done.12, ...), custom_call_target="tpu_custom_call" | custom-call | flops 1 | bytes 1 | tf_op jit(solution)/shard_map/input_grad/input_grad/pallas_call | solution.py:30
  55.7 1.6 %outer.1 = (f32[64,1024]{1,0:T(8,128)}, f32[64,1024]{1,0:T(8,128)}, bf16[8,64,1024]{2,1,0:T(8,128)(2,1)S(1)}) custom-call(s32[3]{0:T(128)S(1)} %pad_add_fusion.pos, bf16[4,64,1024]{2,1,0:T(8,128)(2,1)S(1)} %all-to-all-done.refs_0_, f32[64,1024]{1,0:T(8,128)S(1)} %bitcast.36, f32[64,1024]{1,0:T(8,128)S(1)} %bitcast.37, ...), custom_call_target="tpu_custom_call" | custom-call | flops 1 | bytes 1 | tf_op jit(solution)/shard_map/outer/outer/pallas_call | solution.py:30
  59.3 6.8 %all-to-all-start.1 = ((bf16[8,64,1024]{2,1,0:T(8,128)(2,1)}), bf16[8,64,1024]{2,1,0:T(8,128)(2,1)}, u32[]{:S(2)}, u32[]{:S(2)}) async-start(bf16[8,64,1024]{2,1,0:T(8,128)(2,1)} %copy-done.14), calls=%async_computation.1 | async-start | bytes 2097152 | tf_op jit(solution)/shard_map/outer/all_to_all | solution.py:263
  66.0 5.1 %collective-permute-start.10 = (bf16[384,1536]{1,0:T(8,128)(2,1)}, bf16[384,1536]{1,0:T(8,128)(2,1)S(1)}, u32[]{:S(2)}, u32[]{:S(2)}) collective-permute-start(bf16[384,1536]{1,0:T(8,128)(2,1)} %copy-done.16), channel_id=1, source_target_pairs={{1,0},{2,1},{3,2},{5,4},{6,5},{7,6},{9,8},{10,9},{11,10},{13,12},{... | collective-permute-start | bytes 3538952 | tf_op jit(solution)/shard_map/input_grad/ppermute | solution.py:155
  71.1 1.9 %collective-permute-start.5 = (bf16[384,1536]{1,0:T(8,128)(2,1)}, bf16[384,1536]{1,0:T(8,128)(2,1)S(1)}, u32[]{:S(2)}, u32[]{:S(2)}) collective-permute-start(bf16[384,1536]{1,0:T(8,128)(2,1)} %get-tuple-element.19), channel_id=1, source_target_pairs={{1,16},{2,17},{3,18},{5,20},{6,21},{7,22},{9,24},{10,25},{11,26},{... | collective-permute-start | bytes 3538952 | tf_op jit(solution)/shard_map/input_grad/ppermute | solution.py:155
  73.2 1.2 %copy-done.15 = bf16[8,64,1024]{2,1,0:T(8,128)(2,1)S(1)} copy-done((bf16[8,64,1024]{2,1,0:T(8,128)(2,1)S(1)}, bf16[8,64,1024]{2,1,0:T(8,128)(2,1)}, u32[]{:S(2)}) %copy-start.15) | copy-done | bytes 1048600
  74.5 3.0 %near_grad.2.refs_5_ = bf16[512,1024]{1,0:T(8,128)(2,1)S(1)} custom-call(s32[3]{0:T(128)S(1)} %pad_add_fusion.pos, bf16[384,4096]{1,0:T(8,128)(2,1)} %bitcast.17, bf16[384,1536]{1,0:T(8,128)(2,1)S(1)} %collective-permute-done.8.refs_1_, bf16[384,1024]{1,0:T(8,128)(2,1)S(1)} %bitcast.25, bf16[384,1024]{1,0:T(8,128)(2,1)S(1)} %copy-done.5, ...), custom_call_target="tpu_custom_call" | custom-call | flops 1 | bytes 1 | tf_op jit(solution)/shard_map/weight_grad/near_grad/pallas_call | solution.py:30
  77.5 3.0 %near_grad.3.refs_4_ = bf16[512,1024]{1,0:T(8,128)(2,1)S(1)} custom-call(s32[3]{0:T(128)S(1)} %pad_add_fusion.pos, bf16[384,4096]{1,0:T(8,128)(2,1)} %bitcast.18, bf16[384,1536]{1,0:T(8,128)(2,1)S(1)} %collective-permute-done.8.refs_1_, bf16[384,1024]{1,0:T(8,128)(2,1)S(1)} %bitcast.26, bf16[384,1024]{1,0:T(8,128)(2,1)S(1)} %copy-done.5, ...), custom_call_target="tpu_custom_call" | custom-call | flops 1 | bytes 1 | tf_op jit(solution)/shard_map/weight_grad/near_grad/pallas_call | solution.py:30
  80.4 2.5 %collective-permute-start.13 = (bf16[512,1024]{1,0:T(8,128)(2,1)S(1)}, bf16[512,1024]{1,0:T(8,128)(2,1)S(1)}, u32[]{:S(2)}, u32[]{:S(2)}) collective-permute-start(bf16[512,1024]{1,0:T(8,128)(2,1)S(1)} %near_grad.3.refs_4_), channel_id=1, source_target_pairs={{0,12},{1,13},{2,14},{3,15},{4,0},{5,1},{6,2},{7,3},{8,4},{9,5},{1... | collective-permute-start | bytes 3145736 | tf_op jit(solution)/shard_map/weight_grad/ppermute | solution.py:155
  83.0 2.8 %far_input_grad.1 = (bf16[384,512]{1,0:T(8,128)(2,1)S(1)}, bf16[384,512]{1,0:T(8,128)(2,1)S(1)}) custom-call(s32[3]{0:T(128)S(1)} %pad_add_fusion.pos, bf16[384,1024]{1,0:T(8,128)(2,1)S(1)} %bitcast.27, bf16[384,1024]{1,0:T(8,128)(2,1)S(1)} %copy-done.5, bf16[512,1024]{1,0:T(8,128)(2,1)} %collective-permute-done.6.refs_4_.refs_2_, ...), custom_call_target="tpu_custom_call" | custom-call | flops 1 | bytes 1 | tf_op jit(solution)/shard_map/input_grad/far_input_grad/pallas_call | solution.py:30
  85.8 6.1 %collective-permute-start.11 = (bf16[384,512]{1,0:T(8,128)(2,1)S(1)}, bf16[384,512]{1,0:T(8,128)(2,1)S(1)}, u32[]{:S(2)}, u32[]{:S(2)}) collective-permute-start(bf16[384,512]{1,0:T(8,128)(2,1)S(1)} %get-tuple-element.24.refs_2_), channel_id=1, source_target_pairs={{1,0},{2,1},{3,2},{5,4},{6,5},{7,6},{9,8},{10,9},{11,10},{13,12},{... | collective-permute-start | bytes 1179656 | tf_op jit(solution)/shard_map/input_grad/ppermute | solution.py:155
  91.9 10.8 %collective-permute-done.10.refs_0_ = bf16[384,1536]{1,0:T(8,128)(2,1)S(1)} collective-permute-done((bf16[384,1536]{1,0:T(8,128)(2,1)}, bf16[384,1536]{1,0:T(8,128)(2,1)S(1)}, u32[]{:S(2)}, u32[]{:S(2)}) %collective-permute-start.10) | collective-permute-done | bytes 1179680 | tf_op jit(solution)/shard_map/input_grad/ppermute | solution.py:155
  102.7 1.9 %collective-permute-start.9 = (bf16[384,512]{1,0:T(8,128)(2,1)S(1)}, bf16[384,512]{1,0:T(8,128)(2,1)S(1)}, u32[]{:S(2)}, u32[]{:S(2)}) collective-permute-start(bf16[384,512]{1,0:T(8,128)(2,1)S(1)} %get-tuple-element.23), channel_id=1, source_target_pairs={{1,16},{2,17},{3,18},{5,20},{6,21},{7,22},{9,24},{10,25},{11,26},{... | collective-permute-start | bytes 1179656 | tf_op jit(solution)/shard_map/input_grad/ppermute | solution.py:155
  104.6 3.3 %collective-permute-done.11.refs_1_ = bf16[384,512]{1,0:T(8,128)(2,1)S(1)} collective-permute-done((bf16[384,512]{1,0:T(8,128)(2,1)S(1)}, bf16[384,512]{1,0:T(8,128)(2,1)S(1)}, u32[]{:S(2)}, u32[]{:S(2)}) %collective-permute-start.11) | collective-permute-done | bytes 393248 | tf_op jit(solution)/shard_map/input_grad/ppermute | solution.py:155
  107.9 2.4 %place.2.refs_2_ = bf16[384,4096]{1,0:T(8,128)(2,1)} custom-call(s32[3]{0:T(128)S(1)} %pad_add_fusion.pos, bf16[384,1536]{1,0:T(8,128)(2,1)S(1)} %collective-permute-done.10.refs_0_, bf16[384,512]{1,0:T(8,128)(2,1)S(1)} %collective-permute-done.11.refs_1_, bf16[384,512]{1,0:T(8,128)(2,1)S(1)} %get-tuple-element.24.refs_2_), custom_call_target="tpu_custom_call" | custom-call | flops 1 | bytes 1 | tf_op jit(solution)/shard_map/assemble/place/pallas_call | solution.py:30
  110.3 2.7 %collective-permute-done.9.refs_1_ = bf16[384,512]{1,0:T(8,128)(2,1)S(1)} collective-permute-done((bf16[384,512]{1,0:T(8,128)(2,1)S(1)}, bf16[384,512]{1,0:T(8,128)(2,1)S(1)}, u32[]{:S(2)}, u32[]{:S(2)}) %collective-permute-start.9) | collective-permute-done | bytes 393248 | tf_op jit(solution)/shard_map/input_grad/ppermute | solution.py:155
  113.0 2.4 %place.3.refs_6_ = bf16[384,4096]{1,0:T(8,128)(2,1)} custom-call(s32[3]{0:T(128)S(1)} %pad_add_fusion.pos, bf16[384,1536]{1,0:T(8,128)(2,1)S(1)} %collective-permute-done.5.refs_0_, bf16[384,512]{1,0:T(8,128)(2,1)S(1)} %collective-permute-done.9.refs_1_, bf16[384,4096]{1,0:T(8,128)(2,1)} %place.2.refs_2_), custom_call_target="tpu_custom_call", output_to_operand_aliasing={{}: (3, {})} | custom-call | flops 1 | bytes 1 | tf_op jit(solution)/shard_map/assemble/place/pallas_call | solution.py:30
  115.4 3.9 %last_grad.1 = bf16[512,1024]{1,0:T(8,128)(2,1)} custom-call(s32[3]{0:T(128)S(1)} %pad_add_fusion.pos, bf16[384,4096]{1,0:T(8,128)(2,1)} %bitcast.19, bf16[384,1536]{1,0:T(8,128)(2,1)S(1)} %collective-permute-done.8.refs_1_, bf16[384,1024]{1,0:T(8,128)(2,1)S(1)} %bitcast.28, bf16[384,1024]{1,0:T(8,128)(2,1)S(1)} %copy-done.5, ...), custom_call_target="tpu_custom_call" | custom-call | flops 1 | bytes 1 | tf_op jit(solution)/shard_map/weight_grad/last_grad/pallas_call | solution.py:30
  119.2 2.3 %copy.16 = bf16[1,512,1024]{2,1,0:T(8,128)(2,1)} copy(bf16[1,512,1024]{2,1,0:T(8,128)(2,1)} %bitcast.15) | data formatting | bytes 2097152
  (56 shorter events, 12.0 us)
Async XLA Ops:
  0.6 24.7 %collective-permute-start.2 = (bf16[512,1024]{1,0:T(8,128)(2,1)}, bf16[512,1024]{1,0:T(8,128)(2,1)S(1)}, u32[]{:S(2)}, u32[]{:S(2)}) collective-permute-start(bf16[512,1024]{1,0:T(8,128)(2,1)} %bitcast.33), channel_id=1, source_target_pairs={{0,4},{1,5},{2,6},{3,7},{4,8},{5,9},{6,10},{7,11},{8,12},{9,13},{1... | collective-permute-start | bytes 3145736 | tf_op jit(solution)/shard_map/gather_weight/ppermute | solution.py:155
  2.8 23.7 %collective-permute-start.1 = (bf16[512,1024]{1,0:T(8,128)(2,1)}, bf16[512,1024]{1,0:T(8,128)(2,1)S(1)}, u32[]{:S(2)}, u32[]{:S(2)}) collective-permute-start(bf16[512,1024]{1,0:T(8,128)(2,1)} %bitcast.34), channel_id=1, source_target_pairs={{0,12},{1,13},{2,14},{3,15},{4,0},{5,1},{6,2},{7,3},{8,4},{9,5},{1... | collective-permute-start | bytes 3145736 | tf_op jit(solution)/shard_map/gather_weight/ppermute | solution.py:155
  4.4 19.6 %collective-permute-start = (bf16[384,1024]{1,0:T(8,128)(2,1)}, bf16[384,1024]{1,0:T(8,128)(2,1)S(1)}, u32[]{:S(2)}, u32[]{:S(2)}) collective-permute-start(bf16[384,1024]{1,0:T(8,128)(2,1)} %bitcast.22), channel_id=1, source_target_pairs={{0,16},{1,17},{2,18},{3,19},{4,20},{5,21},{6,22},{7,23},{8,24},{9,... | collective-permute-start | bytes 2359304 | tf_op jit(solution)/shard_map/pair_swap/ppermute | solution.py:155
  5.7 1.9 %copy-start = (bf16[1,1,384,4096]{3,2,1,0:T(8,128)(2,1)S(1)}, bf16[1,1,384,4096]{3,2,1,0:T(8,128)(2,1)}, u32[]{:S(2)}) copy-start(bf16[1,1,384,4096]{3,2,1,0:T(8,128)(2,1)} %param.7) | copy-start | bytes 9437188
  9.0 1.2 %copy-start.13 = (bf16[1,1,512,1024]{3,2,1,0:T(8,128)(2,1)S(1)}, bf16[1,1,512,1024]{3,2,1,0:T(8,128)(2,1)}, u32[]{:S(2)}) copy-start(bf16[1,1,512,1024]{3,2,1,0:T(8,128)(2,1)} %param.10) | copy-start | bytes 3145732
  11.7 12.2 %collective-permute-start.4 = (bf16[256,1024]{1,0:T(8,128)(2,1)S(1)}, bf16[256,1024]{1,0:T(8,128)(2,1)S(1)}, u32[]{:S(2)}, u32[]{:S(2)}) collective-permute-start(bf16[256,1024]{1,0:T(8,128)(2,1)S(1)} %get-tuple-element.17), channel_id=1, source_target_pairs={{0,32},{32,0},{64,96},{96,64},{128,160},{160,128},{192,224},{224,1... | collective-permute-start | bytes 1572872 | tf_op jit(solution)/shard_map/delta/ppermute | solution.py:225
  13.5 23.4 %collective-permute-start.3 = (bf16[384,512]{1,0:T(8,128)(2,1)S(1)}, bf16[384,512]{1,0:T(8,128)(2,1)}, u32[]{:S(2)}, u32[]{:S(2)}) collective-permute-start(bf16[384,512]{1,0:T(8,128)(2,1)S(1)} %split.2.refs_4_), channel_id=1, source_target_pairs={{0,16},{1,17},{2,18},{3,19},{4,20},{5,21},{6,22},{7,23},{8,24},{9,... | collective-permute-start | bytes 1179656 | tf_op jit(solution)/shard_map/pair_swap/ppermute | solution.py:155
  24.0 4.0 %copy-start.2 = (bf16[384,1024]{1,0:T(8,128)(2,1)}, bf16[384,1024]{1,0:T(8,128)(2,1)S(1)}, u32[]{:S(2)}) copy-start(bf16[384,1024]{1,0:T(8,128)(2,1)S(1)} %collective-permute-done.refs_4_.refs_3_.refs_1_) | copy-start | bytes 2359300
  25.3 2.6 %copy-start.9 = (bf16[512,1024]{1,0:T(8,128)(2,1)}, bf16[512,1024]{1,0:T(8,128)(2,1)S(1)}, u32[]{:S(2)}) copy-start(bf16[512,1024]{1,0:T(8,128)(2,1)S(1)} %collective-permute-done.2.refs_2_.refs_4_) | copy-start | bytes 3145732
  26.5 1.4 %copy-start.11 = (bf16[512,1024]{1,0:T(8,128)(2,1)}, bf16[512,1024]{1,0:T(8,128)(2,1)S(1)}, u32[]{:S(2)}) copy-start(bf16[512,1024]{1,0:T(8,128)(2,1)S(1)} %collective-permute-done.1.refs_3_.refs_5_) | copy-start | bytes 3145732
  27.9 27.8 %all-to-all-start = ((bf16[4,64,1024]{2,1,0:T(8,128)(2,1)}), bf16[4,64,1024]{2,1,0:T(8,128)(2,1)S(1)}, u32[]{:S(2)}, u32[]{:S(2)}) async-start(bf16[4,64,1024]{2,1,0:T(8,128)(2,1)} %bitcast.8), calls=%async_computation | async-start | bytes 1048576 | tf_op jit(solution)/shard_map/delta/all_to_all | solution.py:230
  39.1 1.2 %copy-start.10 = (bf16[512,1024]{1,0:T(8,128)(2,1)S(1)}, bf16[512,1024]{1,0:T(8,128)(2,1)}, u32[]{:S(2)}) copy-start(bf16[512,1024]{1,0:T(8,128)(2,1)} %copy-done.9) | copy-start | bytes 3145732
  40.3 4.6 %copy-start.1 = (bf16[1,1,384,4096]{3,2,1,0:T(8,128)(2,1)S(1)}, bf16[1,1,384,4096]{3,2,1,0:T(8,128)(2,1)}, u32[]{:S(2)}) copy-start(bf16[1,1,384,4096]{3,2,1,0:T(8,128)(2,1)} %param.7) | copy-start | bytes 9437188
  45.0 6.1 %copy-start.4 = (bf16[384,1024]{1,0:T(8,128)(2,1)S(1)}, bf16[384,1024]{1,0:T(8,128)(2,1)}, u32[]{:S(2)}) copy-start(bf16[384,1024]{1,0:T(8,128)(2,1)} %copy-done.2) | copy-start | bytes 2359300
  45.0 6.1 %copy-start.7 = (bf16[1,1,384,1024]{3,2,1,0:T(8,128)(2,1)S(1)}, bf16[1,1,384,1024]{3,2,1,0:T(8,128)(2,1)}, u32[]{:S(2)}) copy-start(bf16[1,1,384,1024]{3,2,1,0:T(8,128)(2,1)} %param.8) | copy-start | bytes 2359300
  45.0 6.1 %copy-start.12 = (bf16[512,1024]{1,0:T(8,128)(2,1)S(1)}, bf16[512,1024]{1,0:T(8,128)(2,1)}, u32[]{:S(2)}) copy-start(bf16[512,1024]{1,0:T(8,128)(2,1)} %copy-done.11) | copy-start | bytes 3145732
  45.0 6.1 %copy-start.17 = (bf16[1,1,512,1024]{3,2,1,0:T(8,128)(2,1)S(1)}, bf16[1,1,512,1024]{3,2,1,0:T(8,128)(2,1)}, u32[]{:S(2)}) copy-start(bf16[1,1,512,1024]{3,2,1,0:T(8,128)(2,1)} %param.9) | copy-start | bytes 3145732
  47.2 26.0 %collective-permute-start.8 = (bf16[384,1536]{1,0:T(8,128)(2,1)}, bf16[384,1536]{1,0:T(8,128)(2,1)S(1)}, u32[]{:S(2)}, u32[]{:S(2)}) collective-permute-start(bf16[384,1536]{1,0:T(8,128)(2,1)} %split.3.refs_5_), channel_id=1, source_target_pairs={{0,16},{1,17},{2,18},{3,19},{4,20},{5,21},{6,22},{7,23},{8,24},{9,... | collective-permute-start | bytes 3538952 | tf_op jit(solution)/shard_map/pair_swap/ppermute | solution.py:155
  48.4 24.6 %collective-permute-start.6 = (bf16[512,1024]{1,0:T(8,128)(2,1)}, bf16[512,1024]{1,0:T(8,128)(2,1)}, u32[]{:S(2)}, u32[]{:S(2)}) collective-permute-start(bf16[512,1024]{1,0:T(8,128)(2,1)} %get-tuple-element.18.refs_1_), channel_id=1, source_target_pairs={{0,4},{1,5},{2,6},{3,7},{4,8},{5,9},{6,10},{7,11},{8,12},{9,13},{1... | collective-permute-start | bytes 3145736 | tf_op jit(solution)/shard_map/far/ppermute | solution.py:155
  49.4 6.3 %copy-start.18 = (f32[1,64,1024]{2,1,0:T(8,128)S(1)}, f32[1,64,1024]{2,1,0:T(8,128)}, u32[]{:S(2)}) copy-start(f32[1,64,1024]{2,1,0:T(8,128)} %param.12) | copy-start | bytes 786436
  49.4 6.3 %copy-start.19 = (f32[1,64,1024]{2,1,0:T(8,128)S(1)}, f32[1,64,1024]{2,1,0:T(8,128)}, u32[]{:S(2)}) copy-start(f32[1,64,1024]{2,1,0:T(8,128)} %param.13) | copy-start | bytes 786436
  49.4 28.0 %collective-permute-start.7 = (bf16[512,1024]{1,0:T(8,128)(2,1)}, bf16[512,1024]{1,0:T(8,128)(2,1)}, u32[]{:S(2)}, u32[]{:S(2)}) collective-permute-start(bf16[512,1024]{1,0:T(8,128)(2,1)} %get-tuple-element.20), channel_id=1, source_target_pairs={{0,12},{1,13},{2,14},{3,15},{4,0},{5,1},{6,2},{7,3},{8,4},{9,5},{1... | collective-permute-start | bytes 3145736 | tf_op jit(solution)/shard_map/far/ppermute | solution.py:155
  59.2 14.0 %copy-start.5 = (bf16[384,1024]{1,0:T(8,128)(2,1)S(1)}, bf16[384,1024]{1,0:T(8,128)(2,1)}, u32[]{:S(2)}) copy-start(bf16[384,1024]{1,0:T(8,128)(2,1)} %copy-done.2) | copy-start | bytes 2359300
  59.3 14.0 %copy-start.8 = (bf16[1,1,384,1024]{3,2,1,0:T(8,128)(2,1)S(1)}, bf16[1,1,384,1024]{3,2,1,0:T(8,128)(2,1)}, u32[]{:S(2)}) copy-start(bf16[1,1,384,1024]{3,2,1,0:T(8,128)(2,1)} %param.8) | copy-start | bytes 2359300
  59.3 60.0 %all-to-all-start.1 = ((bf16[8,64,1024]{2,1,0:T(8,128)(2,1)}), bf16[8,64,1024]{2,1,0:T(8,128)(2,1)}, u32[]{:S(2)}, u32[]{:S(2)}) async-start(bf16[8,64,1024]{2,1,0:T(8,128)(2,1)} %copy-done.14), calls=%async_computation.1 | async-start | bytes 2097152 | tf_op jit(solution)/shard_map/outer/all_to_all | solution.py:263
  66.0 36.6 %collective-permute-start.10 = (bf16[384,1536]{1,0:T(8,128)(2,1)}, bf16[384,1536]{1,0:T(8,128)(2,1)S(1)}, u32[]{:S(2)}, u32[]{:S(2)}) collective-permute-start(bf16[384,1536]{1,0:T(8,128)(2,1)} %copy-done.16), channel_id=1, source_target_pairs={{1,0},{2,1},{3,2},{5,4},{6,5},{7,6},{9,8},{10,9},{11,10},{13,12},{... | collective-permute-start | bytes 3538952 | tf_op jit(solution)/shard_map/input_grad/ppermute | solution.py:155
  71.1 39.2 %collective-permute-start.5 = (bf16[384,1536]{1,0:T(8,128)(2,1)}, bf16[384,1536]{1,0:T(8,128)(2,1)S(1)}, u32[]{:S(2)}, u32[]{:S(2)}) collective-permute-start(bf16[384,1536]{1,0:T(8,128)(2,1)} %get-tuple-element.19), channel_id=1, source_target_pairs={{1,16},{2,17},{3,18},{5,20},{6,21},{7,22},{9,24},{10,25},{11,26},{... | collective-permute-start | bytes 3538952 | tf_op jit(solution)/shard_map/input_grad/ppermute | solution.py:155
  73.2 1.2 %copy-start.15 = (bf16[8,64,1024]{2,1,0:T(8,128)(2,1)S(1)}, bf16[8,64,1024]{2,1,0:T(8,128)(2,1)}, u32[]{:S(2)}) copy-start(bf16[8,64,1024]{2,1,0:T(8,128)(2,1)} %copy-done.14) | copy-start | bytes 3145732
  80.4 34.9 %collective-permute-start.13 = (bf16[512,1024]{1,0:T(8,128)(2,1)S(1)}, bf16[512,1024]{1,0:T(8,128)(2,1)S(1)}, u32[]{:S(2)}, u32[]{:S(2)}) collective-permute-start(bf16[512,1024]{1,0:T(8,128)(2,1)S(1)} %near_grad.3.refs_4_), channel_id=1, source_target_pairs={{0,12},{1,13},{2,14},{3,15},{4,0},{5,1},{6,2},{7,3},{8,4},{9,5},{1... | collective-permute-start | bytes 3145736 | tf_op jit(solution)/shard_map/weight_grad/ppermute | solution.py:155
  83.0 32.4 %collective-permute-start.12 = (bf16[512,1024]{1,0:T(8,128)(2,1)S(1)}, bf16[512,1024]{1,0:T(8,128)(2,1)S(1)}, u32[]{:S(2)}, u32[]{:S(2)}) collective-permute-start(bf16[512,1024]{1,0:T(8,128)(2,1)S(1)} %near_grad.2.refs_5_), channel_id=1, source_target_pairs={{0,4},{1,5},{2,6},{3,7},{4,8},{5,9},{6,10},{7,11},{8,12},{9,13},{1... | collective-permute-start | bytes 3145736 | tf_op jit(solution)/shard_map/weight_grad/ppermute | solution.py:155
  85.8 22.1 %collective-permute-start.11 = (bf16[384,512]{1,0:T(8,128)(2,1)S(1)}, bf16[384,512]{1,0:T(8,128)(2,1)S(1)}, u32[]{:S(2)}, u32[]{:S(2)}) collective-permute-start(bf16[384,512]{1,0:T(8,128)(2,1)S(1)} %get-tuple-element.24.refs_2_), channel_id=1, source_target_pairs={{1,0},{2,1},{3,2},{5,4},{6,5},{7,6},{9,8},{10,9},{11,10},{13,12},{... | collective-permute-start | bytes 1179656 | tf_op jit(solution)/shard_map/input_grad/ppermute | solution.py:155
  102.7 10.3 %collective-permute-start.9 = (bf16[384,512]{1,0:T(8,128)(2,1)S(1)}, bf16[384,512]{1,0:T(8,128)(2,1)S(1)}, u32[]{:S(2)}, u32[]{:S(2)}) collective-permute-start(bf16[384,512]{1,0:T(8,128)(2,1)S(1)} %get-tuple-element.23), channel_id=1, source_target_pairs={{1,16},{2,17},{3,18},{5,20},{6,21},{7,22},{9,24},{10,25},{11,26},{... | collective-permute-start | bytes 1179656 | tf_op jit(solution)/shard_map/input_grad/ppermute | solution.py:155
  (4 other events, 4.2 us)

commit v3 on v2

--- a/solution.py
+++ b/solution.py
@@ -10,7 +10,7 @@
 PARAMS = pltpu.CompilerParams(vmem_limit_bytes=48 * 1024 * 1024)
 
 
-def call(kernel, name, grid, in_specs, out_specs, out_shape, aliases=None, after=()):
+def call(kernel, name, grid, in_specs, out_specs, out_shape, aliases=None, after=(), sems=0):
     inputs, count = len(in_specs), len(after)
 
     def with_after(pos, *refs):
@@ -20,7 +20,7 @@
         with_after,
         grid_spec=pltpu.PrefetchScalarGridSpec(
             num_scalar_prefetch=1, grid=grid, in_specs=list(in_specs) + [pl.BlockSpec(memory_space=pl.ANY)] * count,
-            out_specs=out_specs),
+            out_specs=out_specs, scratch_shapes=[pltpu.SemaphoreType.DMA((sems,))] if sems else []),
         out_shape=out_shape,
         input_output_aliases=aliases or {},
         compiler_params=PARAMS,
@@ -132,6 +132,19 @@
     @pl.when(step == NY - 1)
     def _():
         out_ref[...] = rest[...]
+
+
+def split_kernel(rows, numbers, pos, a_ref, out_ref, sems):
+    first = (1 - pos[0]) * NY
+    moves = []
+    for k, r in enumerate(numbers):
+        at = pl.multiple_of((first + block_of(pos, r)) * rows, rows)
+        moves.append(pltpu.make_async_copy(
+            a_ref.at[:, pl.ds(at, rows)], out_ref.at[:, pl.ds(k * rows, rows)], sems.at[k]))
+    for move in moves:
+        move.start()
+    for move in moves:
+        move.wait()
 
 
 def copy_kernel(pos, part_ref, *refs):
@@ -224,7 +237,7 @@
             )(pos, codes, codes, exps, exps)
             arrived = lax.ppermute(send, "replica", [(i, i ^ 1) for i in range(replicas)])
             pair_sum = call(
-                add_kernel, "add", (2,), [part_rows(half // 2, width)] * 2, part_rows(half // 2, width),
+                add_kernel, "add", (1,), [part_rows(half, width)] * 2, part_rows(half, width),
                 jax.ShapeDtypeStruct((half, width), BF16), after=[w_3, w_1, cot_o],
             )(pos, keep, arrived)
             deltas = lax.all_to_all(
@@ -239,7 +252,12 @@
             up_o = moved(far_up, up)
             down_o = moved(far_down, down)
         with jax.named_scope("pair_swap"):
-            send, act_o = swapped_blocks((lambda i: 2 * i + 1 - 5 * (i // 2), 3), [far_up])
+            anywhere = pl.BlockSpec(memory_space=pl.ANY)
+            send = call(
+                lambda *refs: split_kernel(rows, (1, 3, 0), *refs), "split", (1,), [anywhere], anywhere,
+                jax.ShapeDtypeStruct((tok, 3 * rows), BF16), after=[far_up], sems=3,
+            )(pos, act)
+            act_o = moved(send, swap)
         with jax.named_scope("input_grad"):
             shift = lambda x, y, s: (x, y, s - 1)
             flip = lambda x, y, s: (x + 1, y, s - 1)
@@ -273,12 +291,13 @@
             sent_other_2, sent_own_2 = moved(other, flip, 1), moved(own, shift, 1)
         with jax.named_scope("assemble"):
             sent = place(sent_own, sent_own_2, False, [own])
-            sent = place(sent_other, sent_other_2, True, [], sent)
         with jax.named_scope("weight_grad"):
             grad = call(
                 last_grad_kernel, "last_grad", (1,), blocks(0, 2) + [whole((rows, width))] * 2,
                 whole((rows, width)), jax.ShapeDtypeStruct((rows, width), BF16), after=[sent],
             )(pos, act, act_o, cot, cot_o, near_1, near_3)
+        with jax.named_scope("assemble"):
+            sent = place(sent_other, sent_other_2, True, [grad], sent)
         return (sent[None, None], grad[None, None], mom_new[None], mas_new[None], synced[None])
 
     placed = (

time: 122 us -> 120 us (0.984)
  waiting for transfers between devices: 29.7 us -> 26.9 us
    ppermute x13, waiting for transfers between devices: 19.5 us -> 16.7 us  [moved(): return lax.ppermute(value, ('dp', 'section'), pairs)]
    unnamed x42 -> x44, local copies, waits for them, and re-layouts: 13 us -> 14.2 us
  transfers between devices with their start and end apart: 16 -> 16, of which waited for: 7 -> 6; matrix products, arithmetic and copies ran while one was open for 1% -> 1% of each run, Pallas kernels for 28% -> 28%
where the time goes in v3:
time: 120 us; the launch traced here: 119 us
  starting transfers between devices  44.1 us (37%)
  Pallas kernels  33.2 us (28%)
  waiting for transfers between devices  26.9 us (22%)
  local copies, waits for them, and re-layouts  14.2 us (12%)
    pallas_call x13, Pallas kernels, call(): return lambda *operands: run(*operands, *after)  33.2 us
    ppermute x13, starting transfers between devices, moved(): return lax.ppermute(value, ('dp', 'section'), pairs)  26.8 us
    ppermute x13, waiting for transfers between devices, moved(): return lax.ppermute(value, ('dp', 'section'), pairs)  16.7 us
    unnamed x44, local copies, waits for them, and re-layouts  14.2 us
    ppermute x1, waiting for transfers between devices, body(): lax.ppermute(send, 'replica', [(i, i ^ 1) for i in range(replicas)])  10.3 us
    all_to_all x1, starting transfers between devices, body(): lax.all_to_all(pair_sum.reshape(replicas // 2, share, width), 'replica',...  8.85 us
    all_to_all x1, starting transfers between devices, body(): synced = lax.all_to_all(to_sync, 'replica', 0, 0).reshape(rows, width)  6.77 us
  transfers between devices with their start and end apart: 16, of which 6 were waited for; matrix products, arithmetic and copies ran while one was open for 1% of the time, Pallas kernels for 28%

profile of v3, /device:TPU:1, one launch (start us, length us, event | category | flops | bytes accessed | tf_op | source)
XLA Modules:
  0.0 119.4 jit_solution(17644442157745885330)
XLA Ops:
  0.6 2.2 %collective-permute-start.2 = (bf16[512,1024]{1,0:T(8,128)(2,1)}, bf16[512,1024]{1,0:T(8,128)(2,1)S(1)}, u32[]{:S(2)}, u32[]{:S(2)}) collective-permute-start(bf16[512,1024]{1,0:T(8,128)(2,1)} %bitcast.34), channel_id=1, source_target_pairs={{0,4},{1,5},{2,6},{3,7},{4,8},{5,9},{6,10},{7,11},{8,12},{9,13},{1... | collective-permute-start | bytes 3145736 | tf_op jit(solution)/shard_map/gather_weight/ppermute | solution.py:168
  2.8 1.5 %collective-permute-start.1 = (bf16[512,1024]{1,0:T(8,128)(2,1)}, bf16[512,1024]{1,0:T(8,128)(2,1)S(1)}, u32[]{:S(2)}, u32[]{:S(2)}) collective-permute-start(bf16[512,1024]{1,0:T(8,128)(2,1)} %bitcast.35), channel_id=1, source_target_pairs={{0,12},{1,13},{2,14},{3,15},{4,0},{5,1},{6,2},{7,3},{8,4},{9,5},{1... | collective-permute-start | bytes 3145736 | tf_op jit(solution)/shard_map/gather_weight/ppermute | solution.py:168
  5.7 1.9 %copy-done = bf16[1,1,384,4096]{3,2,1,0:T(8,128)(2,1)S(1)} copy-done((bf16[1,1,384,4096]{3,2,1,0:T(8,128)(2,1)S(1)}, bf16[1,1,384,4096]{3,2,1,0:T(8,128)(2,1)}, u32[]{:S(2)}) %copy-start) | copy-done | bytes 3145752
  10.2 1.5 %delta.1 = (bf16[256,1024]{1,0:T(8,128)(2,1)S(1)}, bf16[256,1024]{1,0:T(8,128)(2,1)S(1)}) custom-call(s32[3]{0:T(128)S(1)} %pad_add_fusion.pos, bf16[512,1024]{1,0:T(8,128)(2,1)S(1)} %bitcast.29, bf16[512,1024]{1,0:T(8,128)(2,1)S(1)} %bitcast.30, s32[512,8]{1,0:T(8,128)S(1)} %bitcast.32, s32[512,8]{1,0:T(8,128)S(1)} %bitcast.33, ...), custom_call_target="tpu_custom_call" | custom-call | flops 1 | bytes 1 | tf_op jit(solution)/shard_map/delta/delta/pallas_call | solution.py:30
  11.7 1.7 %collective-permute-start.4 = (bf16[256,1024]{1,0:T(8,128)(2,1)S(1)}, bf16[256,1024]{1,0:T(8,128)(2,1)S(1)}, u32[]{:S(2)}, u32[]{:S(2)}) collective-permute-start(bf16[256,1024]{1,0:T(8,128)(2,1)S(1)} %get-tuple-element.17), channel_id=1, source_target_pairs={{0,32},{32,0},{64,96},{96,64},{128,160},{160,128},{192,224},{224,1... | collective-permute-start | bytes 1572872 | tf_op jit(solution)/shard_map/delta/ppermute | solution.py:238
  13.7 10.3 %collective-permute-done.4.refs_1_ = bf16[256,1024]{1,0:T(8,128)(2,1)S(1)} collective-permute-done((bf16[256,1024]{1,0:T(8,128)(2,1)S(1)}, bf16[256,1024]{1,0:T(8,128)(2,1)S(1)}, u32[]{:S(2)}, u32[]{:S(2)}) %collective-permute-start.4) | collective-permute-done | bytes 524320 | tf_op jit(solution)/shard_map/delta/ppermute | solution.py:238
  24.0 1.4 %collective-permute-done.2.refs_2_.refs_4_ = bf16[512,1024]{1,0:T(8,128)(2,1)S(1)} collective-permute-done((bf16[512,1024]{1,0:T(8,128)(2,1)}, bf16[512,1024]{1,0:T(8,128)(2,1)S(1)}, u32[]{:S(2)}, u32[]{:S(2)}) %collective-permute-start.2) | collective-permute-done | bytes 1048608 | tf_op jit(solution)/shard_map/gather_weight/ppermute | solution.py:168
  26.5 1.5 %add.15.refs_6_ = bf16[256,1024]{1,0:T(8,128)(2,1)} custom-call(s32[3]{0:T(128)S(1)} %pad_add_fusion.pos, bf16[256,1024]{1,0:T(8,128)(2,1)S(1)} %get-tuple-element.16.refs_0_, bf16[256,1024]{1,0:T(8,128)(2,1)S(1)} %collective-permute-done.4.refs_1_, bf16[512,1024]{1,0:T(8,128)(2,1)S(1)} %collective-permute-done.2.refs_2_.refs_4_, ...), custom_call_target="tpu_custom_call" | custom-call | flops 1 | bytes 1 | tf_op jit(solution)/shard_map/delta/add/pallas_call | solution.py:30
  28.0 8.8 %all-to-all-start = ((bf16[4,64,1024]{2,1,0:T(8,128)(2,1)}), bf16[4,64,1024]{2,1,0:T(8,128)(2,1)S(1)}, u32[]{:S(2)}, u32[]{:S(2)}) async-start(bf16[4,64,1024]{2,1,0:T(8,128)(2,1)} %bitcast.8), calls=%async_computation | async-start | bytes 1048576 | tf_op jit(solution)/shard_map/delta/all_to_all | solution.py:243
  39.1 1.2 %copy-done.10 = bf16[512,1024]{1,0:T(8,128)(2,1)S(1)} copy-done((bf16[512,1024]{1,0:T(8,128)(2,1)S(1)}, bf16[512,1024]{1,0:T(8,128)(2,1)}, u32[]{:S(2)}) %copy-start.10) | copy-done | bytes 1048600
  40.3 4.6 %far_grad.1 = (bf16[512,1024]{1,0:T(8,128)(2,1)}, bf16[512,1024]{1,0:T(8,128)(2,1)}) custom-call(s32[3]{0:T(128)S(1)} %pad_add_fusion.pos, bf16[384,4096]{1,0:T(8,128)(2,1)} %bitcast.16, bf16[384,512]{1,0:T(8,128)(2,1)} %collective-permute-done.3.refs_1_, bf16[384,1024]{1,0:T(8,128)(2,1)S(1)} %bitcast.23, bf16[384,1024]{1,0:T(8,128)(2,1)S(1)} %copy-done.3, ...), custom_call_target="tpu_custom_call" | custom-call | flops 1 | bytes 1 | tf_op jit(solution)/shard_map/far/far_grad/pallas_call | solution.py:30
  45.0 1.6 %split.3.refs_5_ = bf16[384,1536]{1,0:T(8,128)(2,1)} custom-call(s32[3]{0:T(128)S(1)} %pad_add_fusion.pos, bf16[384,4096]{1,0:T(8,128)(2,1)S(1)} %bitcast.21, bf16[512,1024]{1,0:T(8,128)(2,1)} %get-tuple-element.18.refs_1_), custom_call_target="tpu_custom_call" | custom-call | flops 1 | bytes 1 | tf_op jit(solution)/shard_map/pair_swap/split/pallas_call | solution.py:30
  46.6 1.3 %collective-permute-start.8 = (bf16[384,1536]{1,0:T(8,128)(2,1)}, bf16[384,1536]{1,0:T(8,128)(2,1)S(1)}, u32[]{:S(2)}, u32[]{:S(2)}) collective-permute-start(bf16[384,1536]{1,0:T(8,128)(2,1)} %split.3.refs_5_), channel_id=1, source_target_pairs={{0,16},{1,17},{2,18},{3,19},{4,20},{5,21},{6,22},{7,23},{8,24},{9,... | collective-permute-start | bytes 3538952 | tf_op jit(solution)/shard_map/pair_swap/ppermute | solution.py:168
  48.9 1.7 %collective-permute-start.7 = (bf16[512,1024]{1,0:T(8,128)(2,1)}, bf16[512,1024]{1,0:T(8,128)(2,1)}, u32[]{:S(2)}, u32[]{:S(2)}) collective-permute-start(bf16[512,1024]{1,0:T(8,128)(2,1)} %get-tuple-element.20), channel_id=1, source_target_pairs={{0,12},{1,13},{2,14},{3,15},{4,0},{5,1},{6,2},{7,3},{8,4},{9,5},{1... | collective-permute-start | bytes 3145736 | tf_op jit(solution)/shard_map/far/ppermute | solution.py:168
  50.6 4.5 %input_grad.1 = (bf16[384,1536]{1,0:T(8,128)(2,1)S(1)}, bf16[384,1536]{1,0:T(8,128)(2,1)}) custom-call(s32[3]{0:T(128)S(1)} %pad_add_fusion.pos, bf16[384,1024]{1,0:T(8,128)(2,1)S(1)} %bitcast.24, bf16[384,1024]{1,0:T(8,128)(2,1)S(1)} %copy-done.4, bf16[512,1024]{1,0:T(8,128)(2,1)S(1)} %bitcast.36, bf16[512,1024]{1,0:T(8,128)(2,1)S(1)} %copy-done.12, ...), custom_call_target="tpu_custom_call" | custom-call | flops 1 | bytes 1 | tf_op jit(solution)/shard_map/input_grad/input_grad/pallas_call | solution.py:30
  55.1 1.6 %outer.1 = (f32[64,1024]{1,0:T(8,128)}, f32[64,1024]{1,0:T(8,128)}, bf16[8,64,1024]{2,1,0:T(8,128)(2,1)S(1)}) custom-call(s32[3]{0:T(128)S(1)} %pad_add_fusion.pos, bf16[4,64,1024]{2,1,0:T(8,128)(2,1)S(1)} %all-to-all-done.refs_0_, f32[64,1024]{1,0:T(8,128)S(1)} %bitcast.37, f32[64,1024]{1,0:T(8,128)S(1)} %bitcast.38, ...), custom_call_target="tpu_custom_call" | custom-call | flops 1 | bytes 1 | tf_op jit(solution)/shard_map/outer/outer/pallas_call | solution.py:30
  58.7 6.8 %all-to-all-start.1 = ((bf16[8,64,1024]{2,1,0:T(8,128)(2,1)}), bf16[8,64,1024]{2,1,0:T(8,128)(2,1)}, u32[]{:S(2)}, u32[]{:S(2)}) async-start(bf16[8,64,1024]{2,1,0:T(8,128)(2,1)} %copy-done.15), calls=%async_computation.1 | async-start | bytes 2097152 | tf_op jit(solution)/shard_map/outer/all_to_all | solution.py:281
  65.4 5.1 %collective-permute-start.10 = (bf16[384,1536]{1,0:T(8,128)(2,1)}, bf16[384,1536]{1,0:T(8,128)(2,1)S(1)}, u32[]{:S(2)}, u32[]{:S(2)}) collective-permute-start(bf16[384,1536]{1,0:T(8,128)(2,1)} %copy-done.17), channel_id=1, source_target_pairs={{1,0},{2,1},{3,2},{5,4},{6,5},{7,6},{9,8},{10,9},{11,10},{13,12},{... | collective-permute-start | bytes 3538952 | tf_op jit(solution)/shard_map/input_grad/ppermute | solution.py:168
  70.5 1.9 %collective-permute-start.5 = (bf16[384,1536]{1,0:T(8,128)(2,1)}, bf16[384,1536]{1,0:T(8,128)(2,1)S(1)}, u32[]{:S(2)}, u32[]{:S(2)}) collective-permute-start(bf16[384,1536]{1,0:T(8,128)(2,1)} %get-tuple-element.19), channel_id=1, source_target_pairs={{1,16},{2,17},{3,18},{5,20},{6,21},{7,22},{9,24},{10,25},{11,26},{... | collective-permute-start | bytes 3538952 | tf_op jit(solution)/shard_map/input_grad/ppermute | solution.py:168
  72.7 1.2 %copy-done.16 = bf16[8,64,1024]{2,1,0:T(8,128)(2,1)S(1)} copy-done((bf16[8,64,1024]{2,1,0:T(8,128)(2,1)S(1)}, bf16[8,64,1024]{2,1,0:T(8,128)(2,1)}, u32[]{:S(2)}) %copy-start.16) | copy-done | bytes 1048600
  73.9 3.0 %near_grad.2.refs_5_ = bf16[512,1024]{1,0:T(8,128)(2,1)S(1)} custom-call(s32[3]{0:T(128)S(1)} %pad_add_fusion.pos, bf16[384,4096]{1,0:T(8,128)(2,1)} %bitcast.17, bf16[384,1536]{1,0:T(8,128)(2,1)S(1)} %collective-permute-done.8.refs_1_, bf16[384,1024]{1,0:T(8,128)(2,1)S(1)} %bitcast.25, bf16[384,1024]{1,0:T(8,128)(2,1)S(1)} %copy-done.5, ...), custom_call_target="tpu_custom_call" | custom-call | flops 1 | bytes 1 | tf_op jit(solution)/shard_map/weight_grad/near_grad/pallas_call | solution.py:30
  76.9 3.0 %near_grad.3.refs_4_ = bf16[512,1024]{1,0:T(8,128)(2,1)S(1)} custom-call(s32[3]{0:T(128)S(1)} %pad_add_fusion.pos, bf16[384,4096]{1,0:T(8,128)(2,1)} %bitcast.18, bf16[384,1536]{1,0:T(8,128)(2,1)S(1)} %collective-permute-done.8.refs_1_, bf16[384,1024]{1,0:T(8,128)(2,1)S(1)} %bitcast.26, bf16[384,1024]{1,0:T(8,128)(2,1)S(1)} %copy-done.5, ...), custom_call_target="tpu_custom_call" | custom-call | flops 1 | bytes 1 | tf_op jit(solution)/shard_map/weight_grad/near_grad/pallas_call | solution.py:30
  79.9 2.6 %collective-permute-start.13 = (bf16[512,1024]{1,0:T(8,128)(2,1)S(1)}, bf16[512,1024]{1,0:T(8,128)(2,1)S(1)}, u32[]{:S(2)}, u32[]{:S(2)}) collective-permute-start(bf16[512,1024]{1,0:T(8,128)(2,1)S(1)} %near_grad.3.refs_4_), channel_id=1, source_target_pairs={{0,12},{1,13},{2,14},{3,15},{4,0},{5,1},{6,2},{7,3},{8,4},{9,5},{1... | collective-permute-start | bytes 3145736 | tf_op jit(solution)/shard_map/weight_grad/ppermute | solution.py:168
  82.5 2.8 %far_input_grad.1 = (bf16[384,512]{1,0:T(8,128)(2,1)S(1)}, bf16[384,512]{1,0:T(8,128)(2,1)S(1)}) custom-call(s32[3]{0:T(128)S(1)} %pad_add_fusion.pos, bf16[384,1024]{1,0:T(8,128)(2,1)S(1)} %bitcast.27, bf16[384,1024]{1,0:T(8,128)(2,1)S(1)} %copy-done.5, bf16[512,1024]{1,0:T(8,128)(2,1)} %collective-permute-done.6.refs_4_.refs_2_, ...), custom_call_target="tpu_custom_call" | custom-call | flops 1 | bytes 1 | tf_op jit(solution)/shard_map/input_grad/far_input_grad/pallas_call | solution.py:30
  85.2 6.2 %collective-permute-start.11 = (bf16[384,512]{1,0:T(8,128)(2,1)S(1)}, bf16[384,512]{1,0:T(8,128)(2,1)S(1)}, u32[]{:S(2)}, u32[]{:S(2)}) collective-permute-start(bf16[384,512]{1,0:T(8,128)(2,1)S(1)} %get-tuple-element.24.refs_2_), channel_id=1, source_target_pairs={{1,0},{2,1},{3,2},{5,4},{6,5},{7,6},{9,8},{10,9},{11,10},{13,12},{... | collective-permute-start | bytes 1179656 | tf_op jit(solution)/shard_map/input_grad/ppermute | solution.py:168
  91.4 10.7 %collective-permute-done.10.refs_0_ = bf16[384,1536]{1,0:T(8,128)(2,1)S(1)} collective-permute-done((bf16[384,1536]{1,0:T(8,128)(2,1)}, bf16[384,1536]{1,0:T(8,128)(2,1)S(1)}, u32[]{:S(2)}, u32[]{:S(2)}) %collective-permute-start.10) | collective-permute-done | bytes 1179680 | tf_op jit(solution)/shard_map/input_grad/ppermute | solution.py:168
  102.1 1.9 %collective-permute-start.9 = (bf16[384,512]{1,0:T(8,128)(2,1)S(1)}, bf16[384,512]{1,0:T(8,128)(2,1)S(1)}, u32[]{:S(2)}, u32[]{:S(2)}) collective-permute-start(bf16[384,512]{1,0:T(8,128)(2,1)S(1)} %get-tuple-element.23), channel_id=1, source_target_pairs={{1,16},{2,17},{3,18},{5,20},{6,21},{7,22},{9,24},{10,25},{11,26},{... | collective-permute-start | bytes 1179656 | tf_op jit(solution)/shard_map/input_grad/ppermute | solution.py:168
  104.0 3.2 %collective-permute-done.11.refs_1_ = bf16[384,512]{1,0:T(8,128)(2,1)S(1)} collective-permute-done((bf16[384,512]{1,0:T(8,128)(2,1)S(1)}, bf16[384,512]{1,0:T(8,128)(2,1)S(1)}, u32[]{:S(2)}, u32[]{:S(2)}) %collective-permute-start.11) | collective-permute-done | bytes 393248 | tf_op jit(solution)/shard_map/input_grad/ppermute | solution.py:168
  107.2 2.4 %place.2.refs_6_.refs_2_ = bf16[384,4096]{1,0:T(8,128)(2,1)} custom-call(s32[3]{0:T(128)S(1)} %pad_add_fusion.pos, bf16[384,1536]{1,0:T(8,128)(2,1)S(1)} %collective-permute-done.10.refs_0_, bf16[384,512]{1,0:T(8,128)(2,1)S(1)} %collective-permute-done.11.refs_1_, bf16[384,512]{1,0:T(8,128)(2,1)S(1)} %get-tuple-element.24.refs_2_), custom_call_target="tpu_custom_call" | custom-call | flops 1 | bytes 1 | tf_op jit(solution)/shard_map/assemble/place/pallas_call | solution.py:30
  109.6 3.9 %last_grad.1.refs_3_ = bf16[512,1024]{1,0:T(8,128)(2,1)} custom-call(s32[3]{0:T(128)S(1)} %pad_add_fusion.pos, bf16[384,4096]{1,0:T(8,128)(2,1)} %bitcast.19, bf16[384,1536]{1,0:T(8,128)(2,1)S(1)} %collective-permute-done.8.refs_1_, bf16[384,1024]{1,0:T(8,128)(2,1)S(1)} %bitcast.28, bf16[384,1024]{1,0:T(8,128)(2,1)S(1)} %copy-done.5, ...), custom_call_target="tpu_custom_call" | custom-call | flops 1 | bytes 1 | tf_op jit(solution)/shard_map/weight_grad/last_grad/pallas_call | solution.py:30
  114.7 2.4 %place.3 = bf16[384,4096]{1,0:T(8,128)(2,1)} custom-call(s32[3]{0:T(128)S(1)} %pad_add_fusion.pos, bf16[384,1536]{1,0:T(8,128)(2,1)S(1)} %collective-permute-done.5.refs_0_, bf16[384,512]{1,0:T(8,128)(2,1)S(1)} %collective-permute-done.9.refs_1_, bf16[384,4096]{1,0:T(8,128)(2,1)} %place.2.refs_6_.refs_2_, ...), custom_call_target="tpu_custom_call", output_to_operand_aliasing={{}: (3, {})} | custom-call | flops 1 | bytes 1 | tf_op jit(solution)/shard_map/assemble/place/pallas_call | solution.py:30
  117.1 2.3 %copy.16 = bf16[1,512,1024]{2,1,0:T(8,128)(2,1)} copy(bf16[1,512,1024]{2,1,0:T(8,128)(2,1)} %bitcast.15) | data formatting | bytes 2097152
  (58 shorter events, 12.1 us)
Async XLA Ops:
  0.6 24.7 %collective-permute-start.2 = (bf16[512,1024]{1,0:T(8,128)(2,1)}, bf16[512,1024]{1,0:T(8,128)(2,1)S(1)}, u32[]{:S(2)}, u32[]{:S(2)}) collective-permute-start(bf16[512,1024]{1,0:T(8,128)(2,1)} %bitcast.34), channel_id=1, source_target_pairs={{0,4},{1,5},{2,6},{3,7},{4,8},{5,9},{6,10},{7,11},{8,12},{9,13},{1... | collective-permute-start | bytes 3145736 | tf_op jit(solution)/shard_map/gather_weight/ppermute | solution.py:168
  2.8 23.7 %collective-permute-start.1 = (bf16[512,1024]{1,0:T(8,128)(2,1)}, bf16[512,1024]{1,0:T(8,128)(2,1)S(1)}, u32[]{:S(2)}, u32[]{:S(2)}) collective-permute-start(bf16[512,1024]{1,0:T(8,128)(2,1)} %bitcast.35), channel_id=1, source_target_pairs={{0,12},{1,13},{2,14},{3,15},{4,0},{5,1},{6,2},{7,3},{8,4},{9,5},{1... | collective-permute-start | bytes 3145736 | tf_op jit(solution)/shard_map/gather_weight/ppermute | solution.py:168
  4.4 19.6 %collective-permute-start = (bf16[384,1024]{1,0:T(8,128)(2,1)}, bf16[384,1024]{1,0:T(8,128)(2,1)S(1)}, u32[]{:S(2)}, u32[]{:S(2)}) collective-permute-start(bf16[384,1024]{1,0:T(8,128)(2,1)} %bitcast.22), channel_id=1, source_target_pairs={{0,16},{1,17},{2,18},{3,19},{4,20},{5,21},{6,22},{7,23},{8,24},{9,... | collective-permute-start | bytes 2359304 | tf_op jit(solution)/shard_map/pair_swap/ppermute | solution.py:168
  5.7 1.9 %copy-start = (bf16[1,1,384,4096]{3,2,1,0:T(8,128)(2,1)S(1)}, bf16[1,1,384,4096]{3,2,1,0:T(8,128)(2,1)}, u32[]{:S(2)}) copy-start(bf16[1,1,384,4096]{3,2,1,0:T(8,128)(2,1)} %param.7) | copy-start | bytes 9437188
  9.0 1.2 %copy-start.13 = (bf16[1,1,512,1024]{3,2,1,0:T(8,128)(2,1)S(1)}, bf16[1,1,512,1024]{3,2,1,0:T(8,128)(2,1)}, u32[]{:S(2)}) copy-start(bf16[1,1,512,1024]{3,2,1,0:T(8,128)(2,1)} %param.10) | copy-start | bytes 3145732
  11.7 12.2 %collective-permute-start.4 = (bf16[256,1024]{1,0:T(8,128)(2,1)S(1)}, bf16[256,1024]{1,0:T(8,128)(2,1)S(1)}, u32[]{:S(2)}, u32[]{:S(2)}) collective-permute-start(bf16[256,1024]{1,0:T(8,128)(2,1)S(1)} %get-tuple-element.17), channel_id=1, source_target_pairs={{0,32},{32,0},{64,96},{96,64},{128,160},{160,128},{192,224},{224,1... | collective-permute-start | bytes 1572872 | tf_op jit(solution)/shard_map/delta/ppermute | solution.py:238
  13.5 23.4 %collective-permute-start.3 = (bf16[384,512]{1,0:T(8,128)(2,1)S(1)}, bf16[384,512]{1,0:T(8,128)(2,1)}, u32[]{:S(2)}, u32[]{:S(2)}) collective-permute-start(bf16[384,512]{1,0:T(8,128)(2,1)S(1)} %split.2.refs_4_), channel_id=1, source_target_pairs={{0,16},{1,17},{2,18},{3,19},{4,20},{5,21},{6,22},{7,23},{8,24},{9,... | collective-permute-start | bytes 1179656 | tf_op jit(solution)/shard_map/pair_swap/ppermute | solution.py:168
  24.0 4.0 %copy-start.2 = (bf16[384,1024]{1,0:T(8,128)(2,1)}, bf16[384,1024]{1,0:T(8,128)(2,1)S(1)}, u32[]{:S(2)}) copy-start(bf16[384,1024]{1,0:T(8,128)(2,1)S(1)} %collective-permute-done.refs_4_.refs_3_.refs_1_) | copy-start | bytes 2359300
  25.3 2.6 %copy-start.9 = (bf16[512,1024]{1,0:T(8,128)(2,1)}, bf16[512,1024]{1,0:T(8,128)(2,1)S(1)}, u32[]{:S(2)}) copy-start(bf16[512,1024]{1,0:T(8,128)(2,1)S(1)} %collective-permute-done.2.refs_2_.refs_4_) | copy-start | bytes 3145732
  26.5 1.5 %copy-start.11 = (bf16[512,1024]{1,0:T(8,128)(2,1)}, bf16[512,1024]{1,0:T(8,128)(2,1)S(1)}, u32[]{:S(2)}) copy-start(bf16[512,1024]{1,0:T(8,128)(2,1)S(1)} %collective-permute-done.1.refs_3_.refs_5_) | copy-start | bytes 3145732
  28.0 27.1 %all-to-all-start = ((bf16[4,64,1024]{2,1,0:T(8,128)(2,1)}), bf16[4,64,1024]{2,1,0:T(8,128)(2,1)S(1)}, u32[]{:S(2)}, u32[]{:S(2)}) async-start(bf16[4,64,1024]{2,1,0:T(8,128)(2,1)} %bitcast.8), calls=%async_computation | async-start | bytes 1048576 | tf_op jit(solution)/shard_map/delta/all_to_all | solution.py:243
  40.3 4.6 %copy-start.1 = (bf16[1,1,384,4096]{3,2,1,0:T(8,128)(2,1)S(1)}, bf16[1,1,384,4096]{3,2,1,0:T(8,128)(2,1)}, u32[]{:S(2)}) copy-start(bf16[1,1,384,4096]{3,2,1,0:T(8,128)(2,1)} %param.7) | copy-start | bytes 9437188
  44.9 5.6 %copy-start.4 = (bf16[384,1024]{1,0:T(8,128)(2,1)S(1)}, bf16[384,1024]{1,0:T(8,128)(2,1)}, u32[]{:S(2)}) copy-start(bf16[384,1024]{1,0:T(8,128)(2,1)} %copy-done.2) | copy-start | bytes 2359300
  44.9 5.6 %copy-start.7 = (bf16[1,1,384,1024]{3,2,1,0:T(8,128)(2,1)S(1)}, bf16[1,1,384,1024]{3,2,1,0:T(8,128)(2,1)}, u32[]{:S(2)}) copy-start(bf16[1,1,384,1024]{3,2,1,0:T(8,128)(2,1)} %param.8) | copy-start | bytes 2359300
  44.9 5.6 %copy-start.12 = (bf16[512,1024]{1,0:T(8,128)(2,1)S(1)}, bf16[512,1024]{1,0:T(8,128)(2,1)}, u32[]{:S(2)}) copy-start(bf16[512,1024]{1,0:T(8,128)(2,1)} %copy-done.11) | copy-start | bytes 3145732
  45.0 5.6 %copy-start.18 = (bf16[1,1,512,1024]{3,2,1,0:T(8,128)(2,1)S(1)}, bf16[1,1,512,1024]{3,2,1,0:T(8,128)(2,1)}, u32[]{:S(2)}) copy-start(bf16[1,1,512,1024]{3,2,1,0:T(8,128)(2,1)} %param.9) | copy-start | bytes 3145732
  46.6 26.1 %collective-permute-start.8 = (bf16[384,1536]{1,0:T(8,128)(2,1)}, bf16[384,1536]{1,0:T(8,128)(2,1)S(1)}, u32[]{:S(2)}, u32[]{:S(2)}) collective-permute-start(bf16[384,1536]{1,0:T(8,128)(2,1)} %split.3.refs_5_), channel_id=1, source_target_pairs={{0,16},{1,17},{2,18},{3,19},{4,20},{5,21},{6,22},{7,23},{8,24},{9,... | collective-permute-start | bytes 3538952 | tf_op jit(solution)/shard_map/pair_swap/ppermute | solution.py:168
  47.9 24.6 %collective-permute-start.6 = (bf16[512,1024]{1,0:T(8,128)(2,1)}, bf16[512,1024]{1,0:T(8,128)(2,1)}, u32[]{:S(2)}, u32[]{:S(2)}) collective-permute-start(bf16[512,1024]{1,0:T(8,128)(2,1)} %get-tuple-element.18.refs_1_), channel_id=1, source_target_pairs={{0,4},{1,5},{2,6},{3,7},{4,8},{5,9},{6,10},{7,11},{8,12},{9,13},{1... | collective-permute-start | bytes 3145736 | tf_op jit(solution)/shard_map/far/ppermute | solution.py:168
  48.9 6.2 %copy-start.19 = (f32[1,64,1024]{2,1,0:T(8,128)S(1)}, f32[1,64,1024]{2,1,0:T(8,128)}, u32[]{:S(2)}) copy-start(f32[1,64,1024]{2,1,0:T(8,128)} %param.12) | copy-start | bytes 786436
  48.9 6.2 %copy-start.20 = (f32[1,64,1024]{2,1,0:T(8,128)S(1)}, f32[1,64,1024]{2,1,0:T(8,128)}, u32[]{:S(2)}) copy-start(f32[1,64,1024]{2,1,0:T(8,128)} %param.13) | copy-start | bytes 786436
  48.9 28.0 %collective-permute-start.7 = (bf16[512,1024]{1,0:T(8,128)(2,1)}, bf16[512,1024]{1,0:T(8,128)(2,1)}, u32[]{:S(2)}, u32[]{:S(2)}) collective-permute-start(bf16[512,1024]{1,0:T(8,128)(2,1)} %get-tuple-element.20), channel_id=1, source_target_pairs={{0,12},{1,13},{2,14},{3,15},{4,0},{5,1},{6,2},{7,3},{8,4},{9,5},{1... | collective-permute-start | bytes 3145736 | tf_op jit(solution)/shard_map/far/ppermute | solution.py:168
  58.7 14.0 %copy-start.5 = (bf16[384,1024]{1,0:T(8,128)(2,1)S(1)}, bf16[384,1024]{1,0:T(8,128)(2,1)}, u32[]{:S(2)}) copy-start(bf16[384,1024]{1,0:T(8,128)(2,1)} %copy-done.2) | copy-start | bytes 2359300
  58.7 14.0 %copy-start.8 = (bf16[1,1,384,1024]{3,2,1,0:T(8,128)(2,1)S(1)}, bf16[1,1,384,1024]{3,2,1,0:T(8,128)(2,1)}, u32[]{:S(2)}) copy-start(bf16[1,1,384,1024]{3,2,1,0:T(8,128)(2,1)} %param.8) | copy-start | bytes 2359300
  58.7 58.4 %all-to-all-start.1 = ((bf16[8,64,1024]{2,1,0:T(8,128)(2,1)}), bf16[8,64,1024]{2,1,0:T(8,128)(2,1)}, u32[]{:S(2)}, u32[]{:S(2)}) async-start(bf16[8,64,1024]{2,1,0:T(8,128)(2,1)} %copy-done.15), calls=%async_computation.1 | async-start | bytes 2097152 | tf_op jit(solution)/shard_map/outer/all_to_all | solution.py:281
  65.4 36.6 %collective-permute-start.10 = (bf16[384,1536]{1,0:T(8,128)(2,1)}, bf16[384,1536]{1,0:T(8,128)(2,1)S(1)}, u32[]{:S(2)}, u32[]{:S(2)}) collective-permute-start(bf16[384,1536]{1,0:T(8,128)(2,1)} %copy-done.17), channel_id=1, source_target_pairs={{1,0},{2,1},{3,2},{5,4},{6,5},{7,6},{9,8},{10,9},{11,10},{13,12},{... | collective-permute-start | bytes 3538952 | tf_op jit(solution)/shard_map/input_grad/ppermute | solution.py:168
  70.5 43.0 %collective-permute-start.5 = (bf16[384,1536]{1,0:T(8,128)(2,1)}, bf16[384,1536]{1,0:T(8,128)(2,1)S(1)}, u32[]{:S(2)}, u32[]{:S(2)}) collective-permute-start(bf16[384,1536]{1,0:T(8,128)(2,1)} %get-tuple-element.19), channel_id=1, source_target_pairs={{1,16},{2,17},{3,18},{5,20},{6,21},{7,22},{9,24},{10,25},{11,26},{... | collective-permute-start | bytes 3538952 | tf_op jit(solution)/shard_map/input_grad/ppermute | solution.py:168
  72.7 1.2 %copy-start.16 = (bf16[8,64,1024]{2,1,0:T(8,128)(2,1)S(1)}, bf16[8,64,1024]{2,1,0:T(8,128)(2,1)}, u32[]{:S(2)}) copy-start(bf16[8,64,1024]{2,1,0:T(8,128)(2,1)} %copy-done.15) | copy-start | bytes 3145732
  79.9 29.7 %collective-permute-start.13 = (bf16[512,1024]{1,0:T(8,128)(2,1)S(1)}, bf16[512,1024]{1,0:T(8,128)(2,1)S(1)}, u32[]{:S(2)}, u32[]{:S(2)}) collective-permute-start(bf16[512,1024]{1,0:T(8,128)(2,1)S(1)} %near_grad.3.refs_4_), channel_id=1, source_target_pairs={{0,12},{1,13},{2,14},{3,15},{4,0},{5,1},{6,2},{7,3},{8,4},{9,5},{1... | collective-permute-start | bytes 3145736 | tf_op jit(solution)/shard_map/weight_grad/ppermute | solution.py:168
  82.5 27.2 %collective-permute-start.12 = (bf16[512,1024]{1,0:T(8,128)(2,1)S(1)}, bf16[512,1024]{1,0:T(8,128)(2,1)S(1)}, u32[]{:S(2)}, u32[]{:S(2)}) collective-permute-start(bf16[512,1024]{1,0:T(8,128)(2,1)S(1)} %near_grad.2.refs_5_), channel_id=1, source_target_pairs={{0,4},{1,5},{2,6},{3,7},{4,8},{5,9},{6,10},{7,11},{8,12},{9,13},{1... | collective-permute-start | bytes 3145736 | tf_op jit(solution)/shard_map/weight_grad/ppermute | solution.py:168
  85.2 22.0 %collective-permute-start.11 = (bf16[384,512]{1,0:T(8,128)(2,1)S(1)}, bf16[384,512]{1,0:T(8,128)(2,1)S(1)}, u32[]{:S(2)}, u32[]{:S(2)}) collective-permute-start(bf16[384,512]{1,0:T(8,128)(2,1)S(1)} %get-tuple-element.24.refs_2_), channel_id=1, source_target_pairs={{1,0},{2,1},{3,2},{5,4},{6,5},{7,6},{9,8},{10,9},{11,10},{13,12},{... | collective-permute-start | bytes 1179656 | tf_op jit(solution)/shard_map/input_grad/ppermute | solution.py:168
  102.1 11.4 %collective-permute-start.9 = (bf16[384,512]{1,0:T(8,128)(2,1)S(1)}, bf16[384,512]{1,0:T(8,128)(2,1)S(1)}, u32[]{:S(2)}, u32[]{:S(2)}) collective-permute-start(bf16[384,512]{1,0:T(8,128)(2,1)S(1)} %get-tuple-element.23), channel_id=1, source_target_pairs={{1,16},{2,17},{3,18},{5,20},{6,21},{7,22},{9,24},{10,25},{11,26},{... | collective-permute-start | bytes 1179656 | tf_op jit(solution)/shard_map/input_grad/ppermute | solution.py:168
  113.5 1.2 %copy-start.14 = (bf16[512,1024]{1,0:T(8,128)(2,1)S(1)}, bf16[512,1024]{1,0:T(8,128)(2,1)}, u32[]{:S(2)}) copy-start(bf16[512,1024]{1,0:T(8,128)(2,1)} %last_grad.1.refs_3_) | copy-start | bytes 3145732
  (5 other events, 5.5 us)

commit v4 on v3

--- a/solution.py
+++ b/solution.py
@@ -208,16 +208,16 @@
             )(pos, act, act_o, cot, cot_o, arrived)
             return part, moved(part, up if r == 1 else down)
 
-        def place(most, rest, flip, after, base=None):
-            number = lambda i: i + i // 2 - i // 3 * 2
+        def place(parts, flip, numbers, after, base=None):
+            number = lambda i: numbers[0] if len(numbers) == 1 else i + i // 2 - i // 3 * 2
             at = lambda i, pos: (0, (1 - pos[0] if flip else pos[0]) * NY + block_of(pos, number(i)))
+            specs = [pl.BlockSpec((tok, rows), lambda i, pos: (0, jnp.minimum(i, NY - 2))), whole((tok, rows))]
             return call(
-                place_kernel, "place", (NY,),
-                [pl.BlockSpec((tok, rows), lambda i, pos: (0, jnp.minimum(i, NY - 2))), whole((tok, rows))]
-                + ([pl.BlockSpec(memory_space=pl.ANY)] if base is not None else []),
+                place_kernel if len(parts) == 2 else copy_kernel, "place", (len(numbers),),
+                specs[:len(parts)] + ([pl.BlockSpec(memory_space=pl.ANY)] if base is not None else []),
                 pl.BlockSpec((tok, rows), at), jax.ShapeDtypeStruct(act.shape, BF16),
-                {3: 0} if base is not None else None, after=after,
-            )(pos, most, rest, *([base] if base is not None else []))
+                {len(parts) + 1: 0} if base is not None else None, after=after,
+            )(pos, *parts, *([base] if base is not None else []))
 
         with jax.named_scope("pair_swap"):
             send, act_2 = swapped_blocks((lambda i: 2, 1), [])
@@ -290,14 +290,15 @@
             )(pos, cot, cot_o, up_o, down_o)
             sent_other_2, sent_own_2 = moved(other, flip, 1), moved(own, shift, 1)
         with jax.named_scope("assemble"):
-            sent = place(sent_own, sent_own_2, False, [own])
+            sent = place([sent_other], True, (0, 1, 3), [own])
         with jax.named_scope("weight_grad"):
             grad = call(
                 last_grad_kernel, "last_grad", (1,), blocks(0, 2) + [whole((rows, width))] * 2,
                 whole((rows, width)), jax.ShapeDtypeStruct((rows, width), BF16), after=[sent],
             )(pos, act, act_o, cot, cot_o, near_1, near_3)
         with jax.named_scope("assemble"):
-            sent = place(sent_other, sent_other_2, True, [grad], sent)
+            sent = place([sent_own, sent_own_2], False, (0, 1, 3, 2), [grad], sent)
+            sent = place([sent_other_2], True, (2,), [], sent)
         return (sent[None, None], grad[None, None], mom_new[None], mas_new[None], synced[None])
 
     placed = (

time: 120 us -> 120 us (level)
  the two profiles are of different devices: /device:TPU:1 before, /device:TPU:4 now
where the time goes in v4:
time: 120 us; the launch traced here: 119 us
  starting transfers between devices  40.1 us (33%)
  Pallas kernels  34.4 us (29%)
  waiting for transfers between devices  29.2 us (24%)
  local copies, waits for them, and re-layouts  14.2 us (12%)
    pallas_call x14, Pallas kernels, call(): return lambda *operands: run(*operands, *after)  34.4 us
    ppermute x13, starting transfers between devices, moved(): return lax.ppermute(value, ('dp', 'section'), pairs)  22.3 us
    ppermute x13, waiting for transfers between devices, moved(): return lax.ppermute(value, ('dp', 'section'), pairs)  18.8 us
    unnamed x44, local copies, waits for them, and re-layouts  14.2 us
    ppermute x1, waiting for transfers between devices, body(): lax.ppermute(send, 'replica', [(i, i ^ 1) for i in range(replicas)])  10.4 us
    all_to_all x1, starting transfers between devices, body(): lax.all_to_all(pair_sum.reshape(replicas // 2, share, width), 'replica',...  8.47 us
    all_to_all x1, starting transfers between devices, body(): synced = lax.all_to_all(to_sync, 'replica', 0, 0).reshape(rows, width)  7.34 us
  transfers between devices with their start and end apart: 16, of which 8 were waited for; matrix products, arithmetic and copies ran while one was open for 1% of the time, Pallas kernels for 29%

profile of v4, /device:TPU:4, one launch (start us, length us, event | category | flops | bytes accessed | tf_op | source)
XLA Modules:
  0.0 118.8 jit_solution(5740855077162812137)
XLA Ops:
  0.6 1.7 %collective-permute-start.2 = (bf16[512,1024]{1,0:T(8,128)(2,1)}, bf16[512,1024]{1,0:T(8,128)(2,1)S(1)}, u32[]{:S(2)}, u32[]{:S(2)}) collective-permute-start(bf16[512,1024]{1,0:T(8,128)(2,1)} %bitcast.34), channel_id=1, source_target_pairs={{0,4},{1,5},{2,6},{3,7},{4,8},{5,9},{6,10},{7,11},{8,12},{9,13},{1... | collective-permute-start | bytes 3145736 | tf_op jit(solution)/shard_map/gather_weight/ppermute | solution.py:168
  2.3 1.7 %collective-permute-start.3 = (bf16[512,1024]{1,0:T(8,128)(2,1)}, bf16[512,1024]{1,0:T(8,128)(2,1)S(1)}, u32[]{:S(2)}, u32[]{:S(2)}) collective-permute-start(bf16[512,1024]{1,0:T(8,128)(2,1)} %bitcast.35), channel_id=1, source_target_pairs={{0,12},{1,13},{2,14},{3,15},{4,0},{5,1},{6,2},{7,3},{8,4},{9,5},{1... | collective-permute-start | bytes 3145736 | tf_op jit(solution)/shard_map/gather_weight/ppermute | solution.py:168
  5.2 1.9 %copy-done = bf16[1,1,384,4096]{3,2,1,0:T(8,128)(2,1)S(1)} copy-done((bf16[1,1,384,4096]{3,2,1,0:T(8,128)(2,1)S(1)}, bf16[1,1,384,4096]{3,2,1,0:T(8,128)(2,1)}, u32[]{:S(2)}) %copy-start) | copy-done | bytes 3145752
  9.8 1.5 %delta.1 = (bf16[256,1024]{1,0:T(8,128)(2,1)S(1)}, bf16[256,1024]{1,0:T(8,128)(2,1)S(1)}) custom-call(s32[3]{0:T(128)S(1)} %pad_add_fusion.pos, bf16[512,1024]{1,0:T(8,128)(2,1)S(1)} %bitcast.29, bf16[512,1024]{1,0:T(8,128)(2,1)S(1)} %bitcast.30, s32[512,8]{1,0:T(8,128)S(1)} %bitcast.32, s32[512,8]{1,0:T(8,128)S(1)} %bitcast.33, ...), custom_call_target="tpu_custom_call" | custom-call | flops 1 | bytes 1 | tf_op jit(solution)/shard_map/delta/delta/pallas_call | solution.py:30
  11.3 2.0 %collective-permute-start.4 = (bf16[256,1024]{1,0:T(8,128)(2,1)S(1)}, bf16[256,1024]{1,0:T(8,128)(2,1)S(1)}, u32[]{:S(2)}, u32[]{:S(2)}) collective-permute-start(bf16[256,1024]{1,0:T(8,128)(2,1)S(1)} %get-tuple-element.17), channel_id=1, source_target_pairs={{0,32},{32,0},{64,96},{96,64},{128,160},{160,128},{192,224},{224,1... | collective-permute-start | bytes 1572872 | tf_op jit(solution)/shard_map/delta/ppermute | solution.py:238
  14.1 10.4 %collective-permute-done.4.refs_1_ = bf16[256,1024]{1,0:T(8,128)(2,1)S(1)} collective-permute-done((bf16[256,1024]{1,0:T(8,128)(2,1)S(1)}, bf16[256,1024]{1,0:T(8,128)(2,1)S(1)}, u32[]{:S(2)}, u32[]{:S(2)}) %collective-permute-start.4) | collective-permute-done | bytes 524320 | tf_op jit(solution)/shard_map/delta/ppermute | solution.py:238
  24.6 2.5 %collective-permute-done.2.refs_2_.refs_4_ = bf16[512,1024]{1,0:T(8,128)(2,1)S(1)} collective-permute-done((bf16[512,1024]{1,0:T(8,128)(2,1)}, bf16[512,1024]{1,0:T(8,128)(2,1)S(1)}, u32[]{:S(2)}, u32[]{:S(2)}) %collective-permute-start.2) | collective-permute-done | bytes 1048608 | tf_op jit(solution)/shard_map/gather_weight/ppermute | solution.py:168
  27.1 1.5 %add.15.refs_6_ = bf16[256,1024]{1,0:T(8,128)(2,1)} custom-call(s32[3]{0:T(128)S(1)} %pad_add_fusion.pos, bf16[256,1024]{1,0:T(8,128)(2,1)S(1)} %get-tuple-element.16.refs_0_, bf16[256,1024]{1,0:T(8,128)(2,1)S(1)} %collective-permute-done.4.refs_1_, bf16[512,1024]{1,0:T(8,128)(2,1)S(1)} %collective-permute-done.2.refs_2_.refs_4_, ...), custom_call_target="tpu_custom_call" | custom-call | flops 1 | bytes 1 | tf_op jit(solution)/shard_map/delta/add/pallas_call | solution.py:30
  28.6 8.5 %all-to-all-start = ((bf16[4,64,1024]{2,1,0:T(8,128)(2,1)}), bf16[4,64,1024]{2,1,0:T(8,128)(2,1)S(1)}, u32[]{:S(2)}, u32[]{:S(2)}) async-start(bf16[4,64,1024]{2,1,0:T(8,128)(2,1)} %bitcast.8), calls=%async_computation | async-start | bytes 1048576 | tf_op jit(solution)/shard_map/delta/all_to_all | solution.py:243
  40.6 4.6 %far_grad.1 = (bf16[512,1024]{1,0:T(8,128)(2,1)}, bf16[512,1024]{1,0:T(8,128)(2,1)}) custom-call(s32[3]{0:T(128)S(1)} %pad_add_fusion.pos, bf16[384,4096]{1,0:T(8,128)(2,1)} %bitcast.16, bf16[384,512]{1,0:T(8,128)(2,1)} %collective-permute-done.1.refs_1_, bf16[384,1024]{1,0:T(8,128)(2,1)S(1)} %bitcast.23, bf16[384,1024]{1,0:T(8,128)(2,1)S(1)} %copy-done.3, ...), custom_call_target="tpu_custom_call" | custom-call | flops 1 | bytes 1 | tf_op jit(solution)/shard_map/far/far_grad/pallas_call | solution.py:30
  45.3 1.6 %split.3.refs_5_ = bf16[384,1536]{1,0:T(8,128)(2,1)} custom-call(s32[3]{0:T(128)S(1)} %pad_add_fusion.pos, bf16[384,4096]{1,0:T(8,128)(2,1)S(1)} %bitcast.21, bf16[512,1024]{1,0:T(8,128)(2,1)} %get-tuple-element.18.refs_1_), custom_call_target="tpu_custom_call" | custom-call | flops 1 | bytes 1 | tf_op jit(solution)/shard_map/pair_swap/split/pallas_call | solution.py:30
  48.1 1.6 %collective-permute-start.5 = (bf16[512,1024]{1,0:T(8,128)(2,1)}, bf16[512,1024]{1,0:T(8,128)(2,1)}, u32[]{:S(2)}, u32[]{:S(2)}) collective-permute-start(bf16[512,1024]{1,0:T(8,128)(2,1)} %get-tuple-element.18.refs_1_), channel_id=1, source_target_pairs={{0,4},{1,5},{2,6},{3,7},{4,8},{5,9},{6,10},{7,11},{8,12},{9,13},{1... | collective-permute-start | bytes 3145736 | tf_op jit(solution)/shard_map/far/ppermute | solution.py:168
  49.7 1.7 %collective-permute-start.6 = (bf16[512,1024]{1,0:T(8,128)(2,1)}, bf16[512,1024]{1,0:T(8,128)(2,1)}, u32[]{:S(2)}, u32[]{:S(2)}) collective-permute-start(bf16[512,1024]{1,0:T(8,128)(2,1)} %get-tuple-element.19), channel_id=1, source_target_pairs={{0,12},{1,13},{2,14},{3,15},{4,0},{5,1},{6,2},{7,3},{8,4},{9,5},{1... | collective-permute-start | bytes 3145736 | tf_op jit(solution)/shard_map/far/ppermute | solution.py:168
  51.4 4.5 %input_grad.1 = (bf16[384,1536]{1,0:T(8,128)(2,1)S(1)}, bf16[384,1536]{1,0:T(8,128)(2,1)}) custom-call(s32[3]{0:T(128)S(1)} %pad_add_fusion.pos, bf16[384,1024]{1,0:T(8,128)(2,1)S(1)} %bitcast.24, bf16[384,1024]{1,0:T(8,128)(2,1)S(1)} %copy-done.4, bf16[512,1024]{1,0:T(8,128)(2,1)S(1)} %bitcast.36, bf16[512,1024]{1,0:T(8,128)(2,1)S(1)} %copy-done.12, ...), custom_call_target="tpu_custom_call" | custom-call | flops 1 | bytes 1 | tf_op jit(solution)/shard_map/input_grad/input_grad/pallas_call | solution.py:30
  55.9 1.6 %outer.1 = (f32[64,1024]{1,0:T(8,128)}, f32[64,1024]{1,0:T(8,128)}, bf16[8,64,1024]{2,1,0:T(8,128)(2,1)S(1)}) custom-call(s32[3]{0:T(128)S(1)} %pad_add_fusion.pos, bf16[4,64,1024]{2,1,0:T(8,128)(2,1)S(1)} %all-to-all-done.refs_0_, f32[64,1024]{1,0:T(8,128)S(1)} %bitcast.37, f32[64,1024]{1,0:T(8,128)S(1)} %bitcast.38, ...), custom_call_target="tpu_custom_call" | custom-call | flops 1 | bytes 1 | tf_op jit(solution)/shard_map/outer/outer/pallas_call | solution.py:30
  59.5 7.3 %all-to-all-start.1 = ((bf16[8,64,1024]{2,1,0:T(8,128)(2,1)}), bf16[8,64,1024]{2,1,0:T(8,128)(2,1)}, u32[]{:S(2)}, u32[]{:S(2)}) async-start(bf16[8,64,1024]{2,1,0:T(8,128)(2,1)} %copy-done.15), calls=%async_computation.1 | async-start | bytes 2097152 | tf_op jit(solution)/shard_map/outer/all_to_all | solution.py:281
  66.9 1.9 %collective-permute-start.11 = (bf16[384,1536]{1,0:T(8,128)(2,1)}, bf16[384,1536]{1,0:T(8,128)(2,1)S(1)}, u32[]{:S(2)}, u32[]{:S(2)}) collective-permute-start(bf16[384,1536]{1,0:T(8,128)(2,1)} %get-tuple-element.24), channel_id=1, source_target_pairs={{1,16},{2,17},{3,18},{5,20},{6,21},{7,22},{9,24},{10,25},{11,26},{... | collective-permute-start | bytes 3538952 | tf_op jit(solution)/shard_map/input_grad/ppermute | solution.py:168
  68.8 3.0 %collective-permute-start.9 = (bf16[384,1536]{1,0:T(8,128)(2,1)}, bf16[384,1536]{1,0:T(8,128)(2,1)S(1)}, u32[]{:S(2)}, u32[]{:S(2)}) collective-permute-start(bf16[384,1536]{1,0:T(8,128)(2,1)} %copy-done.17), channel_id=1, source_target_pairs={{1,0},{2,1},{3,2},{5,4},{6,5},{7,6},{9,8},{10,9},{11,10},{13,12},{... | collective-permute-start | bytes 3538952 | tf_op jit(solution)/shard_map/input_grad/ppermute | solution.py:168
  73.2 2.3 %collective-permute-done.7.refs_1_ = bf16[384,1536]{1,0:T(8,128)(2,1)S(1)} collective-permute-done((bf16[384,1536]{1,0:T(8,128)(2,1)}, bf16[384,1536]{1,0:T(8,128)(2,1)S(1)}, u32[]{:S(2)}, u32[]{:S(2)}) %collective-permute-start.7) | collective-permute-done | bytes 1179680 | tf_op jit(solution)/shard_map/pair_swap/ppermute | solution.py:168
  76.8 3.0 %near_grad.2.refs_5_ = bf16[512,1024]{1,0:T(8,128)(2,1)S(1)} custom-call(s32[3]{0:T(128)S(1)} %pad_add_fusion.pos, bf16[384,4096]{1,0:T(8,128)(2,1)} %bitcast.17, bf16[384,1536]{1,0:T(8,128)(2,1)S(1)} %collective-permute-done.7.refs_1_, bf16[384,1024]{1,0:T(8,128)(2,1)S(1)} %bitcast.25, bf16[384,1024]{1,0:T(8,128)(2,1)S(1)} %copy-done.5, ...), custom_call_target="tpu_custom_call" | custom-call | flops 1 | bytes 1 | tf_op jit(solution)/shard_map/weight_grad/near_grad/pallas_call | solution.py:30
  79.8 3.0 %near_grad.3.refs_4_ = bf16[512,1024]{1,0:T(8,128)(2,1)S(1)} custom-call(s32[3]{0:T(128)S(1)} %pad_add_fusion.pos, bf16[384,4096]{1,0:T(8,128)(2,1)} %bitcast.18, bf16[384,1536]{1,0:T(8,128)(2,1)S(1)} %collective-permute-done.7.refs_1_, bf16[384,1024]{1,0:T(8,128)(2,1)S(1)} %bitcast.26, bf16[384,1024]{1,0:T(8,128)(2,1)S(1)} %copy-done.5, ...), custom_call_target="tpu_custom_call" | custom-call | flops 1 | bytes 1 | tf_op jit(solution)/shard_map/weight_grad/near_grad/pallas_call | solution.py:30
  82.8 3.8 %collective-permute-start.13 = (bf16[512,1024]{1,0:T(8,128)(2,1)S(1)}, bf16[512,1024]{1,0:T(8,128)(2,1)S(1)}, u32[]{:S(2)}, u32[]{:S(2)}) collective-permute-start(bf16[512,1024]{1,0:T(8,128)(2,1)S(1)} %near_grad.3.refs_4_), channel_id=1, source_target_pairs={{0,12},{1,13},{2,14},{3,15},{4,0},{5,1},{6,2},{7,3},{8,4},{9,5},{1... | collective-permute-start | bytes 3145736 | tf_op jit(solution)/shard_map/weight_grad/ppermute | solution.py:168
  86.5 2.8 %far_input_grad.1 = (bf16[384,512]{1,0:T(8,128)(2,1)S(1)}, bf16[384,512]{1,0:T(8,128)(2,1)S(1)}) custom-call(s32[3]{0:T(128)S(1)} %pad_add_fusion.pos, bf16[384,1024]{1,0:T(8,128)(2,1)S(1)} %bitcast.27, bf16[384,1024]{1,0:T(8,128)(2,1)S(1)} %copy-done.5, bf16[512,1024]{1,0:T(8,128)(2,1)} %collective-permute-done.5.refs_4_.refs_2_, ...), custom_call_target="tpu_custom_call" | custom-call | flops 1 | bytes 1 | tf_op jit(solution)/shard_map/input_grad/far_input_grad/pallas_call | solution.py:30
  89.3 1.9 %collective-permute-start.10 = (bf16[384,512]{1,0:T(8,128)(2,1)S(1)}, bf16[384,512]{1,0:T(8,128)(2,1)S(1)}, u32[]{:S(2)}, u32[]{:S(2)}) collective-permute-start(bf16[384,512]{1,0:T(8,128)(2,1)S(1)} %get-tuple-element.23.refs_1_), channel_id=1, source_target_pairs={{1,0},{2,1},{3,2},{5,4},{6,5},{7,6},{9,8},{10,9},{11,10},{13,12},{... | collective-permute-start | bytes 1179656 | tf_op jit(solution)/shard_map/input_grad/ppermute | solution.py:168
  91.2 6.0 %collective-permute-done.11.refs_0_ = bf16[384,1536]{1,0:T(8,128)(2,1)S(1)} collective-permute-done((bf16[384,1536]{1,0:T(8,128)(2,1)}, bf16[384,1536]{1,0:T(8,128)(2,1)S(1)}, u32[]{:S(2)}, u32[]{:S(2)}) %collective-permute-start.11) | collective-permute-done | bytes 1179680 | tf_op jit(solution)/shard_map/input_grad/ppermute | solution.py:168
  97.2 1.9 %collective-permute-start.8 = (bf16[384,512]{1,0:T(8,128)(2,1)S(1)}, bf16[384,512]{1,0:T(8,128)(2,1)S(1)}, u32[]{:S(2)}, u32[]{:S(2)}) collective-permute-start(bf16[384,512]{1,0:T(8,128)(2,1)S(1)} %get-tuple-element.22), channel_id=1, source_target_pairs={{1,16},{2,17},{3,18},{5,20},{6,21},{7,22},{9,24},{10,25},{11,26},{... | collective-permute-start | bytes 1179656 | tf_op jit(solution)/shard_map/input_grad/ppermute | solution.py:168
  99.1 2.2 %place.3.refs_6_.refs_2_ = bf16[384,4096]{1,0:T(8,128)(2,1)} custom-call(s32[3]{0:T(128)S(1)} %pad_add_fusion.pos, bf16[384,1536]{1,0:T(8,128)(2,1)S(1)} %collective-permute-done.11.refs_0_, bf16[384,512]{1,0:T(8,128)(2,1)S(1)} %get-tuple-element.23.refs_1_), custom_call_target="tpu_custom_call" | custom-call | flops 1 | bytes 1 | tf_op jit(solution)/shard_map/assemble/place/pallas_call | solution.py:30
  101.3 3.0 %collective-permute-done.13.refs_5_ = bf16[512,1024]{1,0:T(8,128)(2,1)S(1)} collective-permute-done((bf16[512,1024]{1,0:T(8,128)(2,1)S(1)}, bf16[512,1024]{1,0:T(8,128)(2,1)S(1)}, u32[]{:S(2)}, u32[]{:S(2)}) %collective-permute-start.13) | collective-permute-done | bytes 1048608 | tf_op jit(solution)/shard_map/weight_grad/ppermute | solution.py:168
  104.4 3.4 %collective-permute-done.12.refs_4_ = bf16[512,1024]{1,0:T(8,128)(2,1)S(1)} collective-permute-done((bf16[512,1024]{1,0:T(8,128)(2,1)S(1)}, bf16[512,1024]{1,0:T(8,128)(2,1)S(1)}, u32[]{:S(2)}, u32[]{:S(2)}) %collective-permute-start.12) | collective-permute-done | bytes 1048608 | tf_op jit(solution)/shard_map/weight_grad/ppermute | solution.py:168
  107.8 3.9 %last_grad.1.refs_3_ = bf16[512,1024]{1,0:T(8,128)(2,1)} custom-call(s32[3]{0:T(128)S(1)} %pad_add_fusion.pos, bf16[384,4096]{1,0:T(8,128)(2,1)} %bitcast.19, bf16[384,1536]{1,0:T(8,128)(2,1)S(1)} %collective-permute-done.7.refs_1_, bf16[384,1024]{1,0:T(8,128)(2,1)S(1)} %bitcast.28, bf16[384,1024]{1,0:T(8,128)(2,1)S(1)} %copy-done.5, ...), custom_call_target="tpu_custom_call" | custom-call | flops 1 | bytes 1 | tf_op jit(solution)/shard_map/weight_grad/last_grad/pallas_call | solution.py:30
  112.9 2.4 %place.4.refs_1_ = bf16[384,4096]{1,0:T(8,128)(2,1)} custom-call(s32[3]{0:T(128)S(1)} %pad_add_fusion.pos, bf16[384,1536]{1,0:T(8,128)(2,1)S(1)} %collective-permute-done.9.refs_0_, bf16[384,512]{1,0:T(8,128)(2,1)S(1)} %collective-permute-done.10.refs_1_, bf16[384,4096]{1,0:T(8,128)(2,1)} %place.3.refs_6_.refs_2_, ...), custom_call_target="tpu_custom_call", output_to_operand_aliasing={{}: (3, {})} | custom-call | flops 1 | bytes 1 | tf_op jit(solution)/shard_map/assemble/place/pallas_call | solution.py:30
  116.6 2.3 %copy.18 = bf16[1,512,1024]{2,1,0:T(8,128)(2,1)} copy(bf16[1,512,1024]{2,1,0:T(8,128)(2,1)} %bitcast.15) | data formatting | bytes 2097152
  (59 shorter events, 16.9 us)
Async XLA Ops:
  0.6 26.5 %collective-permute-start.2 = (bf16[512,1024]{1,0:T(8,128)(2,1)}, bf16[512,1024]{1,0:T(8,128)(2,1)S(1)}, u32[]{:S(2)}, u32[]{:S(2)}) collective-permute-start(bf16[512,1024]{1,0:T(8,128)(2,1)} %bitcast.34), channel_id=1, source_target_pairs={{0,4},{1,5},{2,6},{3,7},{4,8},{5,9},{6,10},{7,11},{8,12},{9,13},{1... | collective-permute-start | bytes 3145736 | tf_op jit(solution)/shard_map/gather_weight/ppermute | solution.py:168
  2.3 24.8 %collective-permute-start.3 = (bf16[512,1024]{1,0:T(8,128)(2,1)}, bf16[512,1024]{1,0:T(8,128)(2,1)S(1)}, u32[]{:S(2)}, u32[]{:S(2)}) collective-permute-start(bf16[512,1024]{1,0:T(8,128)(2,1)} %bitcast.35), channel_id=1, source_target_pairs={{0,12},{1,13},{2,14},{3,15},{4,0},{5,1},{6,2},{7,3},{8,4},{9,5},{1... | collective-permute-start | bytes 3145736 | tf_op jit(solution)/shard_map/gather_weight/ppermute | solution.py:168
  3.9 20.7 %collective-permute-start = (bf16[384,1024]{1,0:T(8,128)(2,1)}, bf16[384,1024]{1,0:T(8,128)(2,1)S(1)}, u32[]{:S(2)}, u32[]{:S(2)}) collective-permute-start(bf16[384,1024]{1,0:T(8,128)(2,1)} %bitcast.22), channel_id=1, source_target_pairs={{0,16},{1,17},{2,18},{3,19},{4,20},{5,21},{6,22},{7,23},{8,24},{9,... | collective-permute-start | bytes 2359304 | tf_op jit(solution)/shard_map/pair_swap/ppermute | solution.py:168
  5.2 1.9 %copy-start = (bf16[1,1,384,4096]{3,2,1,0:T(8,128)(2,1)S(1)}, bf16[1,1,384,4096]{3,2,1,0:T(8,128)(2,1)}, u32[]{:S(2)}) copy-start(bf16[1,1,384,4096]{3,2,1,0:T(8,128)(2,1)} %param.7) | copy-start | bytes 9437188
  8.5 1.2 %copy-start.13 = (bf16[1,1,512,1024]{3,2,1,0:T(8,128)(2,1)S(1)}, bf16[1,1,512,1024]{3,2,1,0:T(8,128)(2,1)}, u32[]{:S(2)}) copy-start(bf16[1,1,512,1024]{3,2,1,0:T(8,128)(2,1)} %param.10) | copy-start | bytes 3145732
  11.3 13.2 %collective-permute-start.4 = (bf16[256,1024]{1,0:T(8,128)(2,1)S(1)}, bf16[256,1024]{1,0:T(8,128)(2,1)S(1)}, u32[]{:S(2)}, u32[]{:S(2)}) collective-permute-start(bf16[256,1024]{1,0:T(8,128)(2,1)S(1)} %get-tuple-element.17), channel_id=1, source_target_pairs={{0,32},{32,0},{64,96},{96,64},{128,160},{160,128},{192,224},{224,1... | collective-permute-start | bytes 1572872 | tf_op jit(solution)/shard_map/delta/ppermute | solution.py:238
  13.3 23.8 %collective-permute-start.1 = (bf16[384,512]{1,0:T(8,128)(2,1)S(1)}, bf16[384,512]{1,0:T(8,128)(2,1)}, u32[]{:S(2)}, u32[]{:S(2)}) collective-permute-start(bf16[384,512]{1,0:T(8,128)(2,1)S(1)} %split.2.refs_4_), channel_id=1, source_target_pairs={{0,16},{1,17},{2,18},{3,19},{4,20},{5,21},{6,22},{7,23},{8,24},{9,... | collective-permute-start | bytes 1179656 | tf_op jit(solution)/shard_map/pair_swap/ppermute | solution.py:168
  24.6 4.0 %copy-start.2 = (bf16[384,1024]{1,0:T(8,128)(2,1)}, bf16[384,1024]{1,0:T(8,128)(2,1)S(1)}, u32[]{:S(2)}) copy-start(bf16[384,1024]{1,0:T(8,128)(2,1)S(1)} %collective-permute-done.refs_4_.refs_3_.refs_1_) | copy-start | bytes 2359300
  27.1 1.5 %copy-start.9 = (bf16[512,1024]{1,0:T(8,128)(2,1)}, bf16[512,1024]{1,0:T(8,128)(2,1)S(1)}, u32[]{:S(2)}) copy-start(bf16[512,1024]{1,0:T(8,128)(2,1)S(1)} %collective-permute-done.2.refs_2_.refs_4_) | copy-start | bytes 3145732
  27.1 1.5 %copy-start.11 = (bf16[512,1024]{1,0:T(8,128)(2,1)}, bf16[512,1024]{1,0:T(8,128)(2,1)S(1)}, u32[]{:S(2)}) copy-start(bf16[512,1024]{1,0:T(8,128)(2,1)S(1)} %collective-permute-done.3.refs_3_.refs_5_) | copy-start | bytes 3145732
  28.6 27.3 %all-to-all-start = ((bf16[4,64,1024]{2,1,0:T(8,128)(2,1)}), bf16[4,64,1024]{2,1,0:T(8,128)(2,1)S(1)}, u32[]{:S(2)}, u32[]{:S(2)}) async-start(bf16[4,64,1024]{2,1,0:T(8,128)(2,1)} %bitcast.8), calls=%async_computation | async-start | bytes 1048576 | tf_op jit(solution)/shard_map/delta/all_to_all | solution.py:243
  40.6 4.6 %copy-start.1 = (bf16[1,1,384,4096]{3,2,1,0:T(8,128)(2,1)S(1)}, bf16[1,1,384,4096]{3,2,1,0:T(8,128)(2,1)}, u32[]{:S(2)}) copy-start(bf16[1,1,384,4096]{3,2,1,0:T(8,128)(2,1)} %param.7) | copy-start | bytes 9437188
  45.2 6.2 %copy-start.4 = (bf16[384,1024]{1,0:T(8,128)(2,1)S(1)}, bf16[384,1024]{1,0:T(8,128)(2,1)}, u32[]{:S(2)}) copy-start(bf16[384,1024]{1,0:T(8,128)(2,1)} %copy-done.2) | copy-start | bytes 2359300
  45.2 6.2 %copy-start.7 = (bf16[1,1,384,1024]{3,2,1,0:T(8,128)(2,1)S(1)}, bf16[1,1,384,1024]{3,2,1,0:T(8,128)(2,1)}, u32[]{:S(2)}) copy-start(bf16[1,1,384,1024]{3,2,1,0:T(8,128)(2,1)} %param.8) | copy-start | bytes 2359300
  45.2 6.2 %copy-start.12 = (bf16[512,1024]{1,0:T(8,128)(2,1)S(1)}, bf16[512,1024]{1,0:T(8,128)(2,1)}, u32[]{:S(2)}) copy-start(bf16[512,1024]{1,0:T(8,128)(2,1)} %copy-done.11) | copy-start | bytes 3145732
  45.2 6.1 %copy-start.18 = (bf16[1,1,512,1024]{3,2,1,0:T(8,128)(2,1)S(1)}, bf16[1,1,512,1024]{3,2,1,0:T(8,128)(2,1)}, u32[]{:S(2)}) copy-start(bf16[1,1,512,1024]{3,2,1,0:T(8,128)(2,1)} %param.9) | copy-start | bytes 3145732
  46.8 28.7 %collective-permute-start.7 = (bf16[384,1536]{1,0:T(8,128)(2,1)}, bf16[384,1536]{1,0:T(8,128)(2,1)S(1)}, u32[]{:S(2)}, u32[]{:S(2)}) collective-permute-start(bf16[384,1536]{1,0:T(8,128)(2,1)} %split.3.refs_5_), channel_id=1, source_target_pairs={{0,16},{1,17},{2,18},{3,19},{4,20},{5,21},{6,22},{7,23},{8,24},{9,... | collective-permute-start | bytes 3538952 | tf_op jit(solution)/shard_map/pair_swap/ppermute | solution.py:168
  48.1 25.1 %collective-permute-start.5 = (bf16[512,1024]{1,0:T(8,128)(2,1)}, bf16[512,1024]{1,0:T(8,128)(2,1)}, u32[]{:S(2)}, u32[]{:S(2)}) collective-permute-start(bf16[512,1024]{1,0:T(8,128)(2,1)} %get-tuple-element.18.refs_1_), channel_id=1, source_target_pairs={{0,4},{1,5},{2,6},{3,7},{4,8},{5,9},{6,10},{7,11},{8,12},{9,13},{1... | collective-permute-start | bytes 3145736 | tf_op jit(solution)/shard_map/far/ppermute | solution.py:168
  49.7 6.2 %copy-start.19 = (f32[1,64,1024]{2,1,0:T(8,128)S(1)}, f32[1,64,1024]{2,1,0:T(8,128)}, u32[]{:S(2)}) copy-start(f32[1,64,1024]{2,1,0:T(8,128)} %param.12) | copy-start | bytes 786436
  49.7 6.2 %copy-start.20 = (f32[1,64,1024]{2,1,0:T(8,128)S(1)}, f32[1,64,1024]{2,1,0:T(8,128)}, u32[]{:S(2)}) copy-start(f32[1,64,1024]{2,1,0:T(8,128)} %param.13) | copy-start | bytes 786436
  49.7 30.1 %collective-permute-start.6 = (bf16[512,1024]{1,0:T(8,128)(2,1)}, bf16[512,1024]{1,0:T(8,128)(2,1)}, u32[]{:S(2)}, u32[]{:S(2)}) collective-permute-start(bf16[512,1024]{1,0:T(8,128)(2,1)} %get-tuple-element.19), channel_id=1, source_target_pairs={{0,12},{1,13},{2,14},{3,15},{4,0},{5,1},{6,2},{7,3},{8,4},{9,5},{1... | collective-permute-start | bytes 3145736 | tf_op jit(solution)/shard_map/far/ppermute | solution.py:168
  59.5 16.0 %copy-start.5 = (bf16[384,1024]{1,0:T(8,128)(2,1)S(1)}, bf16[384,1024]{1,0:T(8,128)(2,1)}, u32[]{:S(2)}) copy-start(bf16[384,1024]{1,0:T(8,128)(2,1)} %copy-done.2) | copy-start | bytes 2359300
  59.5 16.0 %copy-start.8 = (bf16[1,1,384,1024]{3,2,1,0:T(8,128)(2,1)S(1)}, bf16[1,1,384,1024]{3,2,1,0:T(8,128)(2,1)}, u32[]{:S(2)}) copy-start(bf16[1,1,384,1024]{3,2,1,0:T(8,128)(2,1)} %param.8) | copy-start | bytes 2359300
  59.5 57.0 %all-to-all-start.1 = ((bf16[8,64,1024]{2,1,0:T(8,128)(2,1)}), bf16[8,64,1024]{2,1,0:T(8,128)(2,1)}, u32[]{:S(2)}, u32[]{:S(2)}) async-start(bf16[8,64,1024]{2,1,0:T(8,128)(2,1)} %copy-done.15), calls=%async_computation.1 | async-start | bytes 2097152 | tf_op jit(solution)/shard_map/outer/all_to_all | solution.py:281
  66.9 30.3 %collective-permute-start.11 = (bf16[384,1536]{1,0:T(8,128)(2,1)}, bf16[384,1536]{1,0:T(8,128)(2,1)S(1)}, u32[]{:S(2)}, u32[]{:S(2)}) collective-permute-start(bf16[384,1536]{1,0:T(8,128)(2,1)} %get-tuple-element.24), channel_id=1, source_target_pairs={{1,16},{2,17},{3,18},{5,20},{6,21},{7,22},{9,24},{10,25},{11,26},{... | collective-permute-start | bytes 3538952 | tf_op jit(solution)/shard_map/input_grad/ppermute | solution.py:168
  68.8 42.9 %collective-permute-start.9 = (bf16[384,1536]{1,0:T(8,128)(2,1)}, bf16[384,1536]{1,0:T(8,128)(2,1)S(1)}, u32[]{:S(2)}, u32[]{:S(2)}) collective-permute-start(bf16[384,1536]{1,0:T(8,128)(2,1)} %copy-done.17), channel_id=1, source_target_pairs={{1,0},{2,1},{3,2},{5,4},{6,5},{7,6},{9,8},{10,9},{11,10},{13,12},{... | collective-permute-start | bytes 3538952 | tf_op jit(solution)/shard_map/input_grad/ppermute | solution.py:168
  75.5 1.2 %copy-start.16 = (bf16[8,64,1024]{2,1,0:T(8,128)(2,1)S(1)}, bf16[8,64,1024]{2,1,0:T(8,128)(2,1)}, u32[]{:S(2)}) copy-start(bf16[8,64,1024]{2,1,0:T(8,128)(2,1)} %copy-done.15) | copy-start | bytes 3145732
  82.8 21.6 %collective-permute-start.13 = (bf16[512,1024]{1,0:T(8,128)(2,1)S(1)}, bf16[512,1024]{1,0:T(8,128)(2,1)S(1)}, u32[]{:S(2)}, u32[]{:S(2)}) collective-permute-start(bf16[512,1024]{1,0:T(8,128)(2,1)S(1)} %near_grad.3.refs_4_), channel_id=1, source_target_pairs={{0,12},{1,13},{2,14},{3,15},{4,0},{5,1},{6,2},{7,3},{8,4},{9,5},{1... | collective-permute-start | bytes 3145736 | tf_op jit(solution)/shard_map/weight_grad/ppermute | solution.py:168
  86.5 21.2 %collective-permute-start.12 = (bf16[512,1024]{1,0:T(8,128)(2,1)S(1)}, bf16[512,1024]{1,0:T(8,128)(2,1)S(1)}, u32[]{:S(2)}, u32[]{:S(2)}) collective-permute-start(bf16[512,1024]{1,0:T(8,128)(2,1)S(1)} %near_grad.2.refs_5_), channel_id=1, source_target_pairs={{0,4},{1,5},{2,6},{3,7},{4,8},{5,9},{6,10},{7,11},{8,12},{9,13},{1... | collective-permute-start | bytes 3145736 | tf_op jit(solution)/shard_map/weight_grad/ppermute | solution.py:168
  89.3 22.3 %collective-permute-start.10 = (bf16[384,512]{1,0:T(8,128)(2,1)S(1)}, bf16[384,512]{1,0:T(8,128)(2,1)S(1)}, u32[]{:S(2)}, u32[]{:S(2)}) collective-permute-start(bf16[384,512]{1,0:T(8,128)(2,1)S(1)} %get-tuple-element.23.refs_1_), channel_id=1, source_target_pairs={{1,0},{2,1},{3,2},{5,4},{6,5},{7,6},{9,8},{10,9},{11,10},{13,12},{... | collective-permute-start | bytes 1179656 | tf_op jit(solution)/shard_map/input_grad/ppermute | solution.py:168
  97.2 18.0 %collective-permute-start.8 = (bf16[384,512]{1,0:T(8,128)(2,1)S(1)}, bf16[384,512]{1,0:T(8,128)(2,1)S(1)}, u32[]{:S(2)}, u32[]{:S(2)}) collective-permute-start(bf16[384,512]{1,0:T(8,128)(2,1)S(1)} %get-tuple-element.22), channel_id=1, source_target_pairs={{1,16},{2,17},{3,18},{5,20},{6,21},{7,22},{9,24},{10,25},{11,26},{... | collective-permute-start | bytes 1179656 | tf_op jit(solution)/shard_map/input_grad/ppermute | solution.py:168
  111.6 1.2 %copy-start.14 = (bf16[512,1024]{1,0:T(8,128)(2,1)S(1)}, bf16[512,1024]{1,0:T(8,128)(2,1)}, u32[]{:S(2)}) copy-start(bf16[512,1024]{1,0:T(8,128)(2,1)} %last_grad.1.refs_3_) | copy-start | bytes 3145732
  (5 other events, 5.5 us)
